TPU v7x, 32 devices: a whole 2x2x4 slice. The times are simulated.
32 devices in a mesh: gx: 4 (over y, core), gy: 8 (over z, x).
Axes of the slice: x: 2, y: 2, z: 4, core: 2. Of those that a mesh axis runs over, the one named last changes fastest.
Arguments:
- volume_sens: float32 [3, 128, 256, 128], P(None, 'gx', 'gy'), may hold values from -6 to 6
- stiffness: float32 [128, 256, 128], P('gx', 'gy'), may hold values from 0.25 to 4
- patch_of_row: int32 [32, 1024, 1], P(('gx', 'gy')), may hold values from 0 to 31; in each aligned block of 1024 rows (0 to 1023, 1024 to 2047, ..., all dimensions but the last counted through in order) at most 128 rows name the same one
- knot_spans: int32 [32, 1024, 2], P(('gx', 'gy')), may hold values from 0 to 60
- span_params: float32 [32, 1024, 2], P(('gx', 'gy')), may hold values from 0 to 1
Outputs:
- adjoint_field: float32 [3, 128, 256, 128], P(None, 'gx', 'gy')
- control_grad: float32 [32, 3, 64, 64], P(('gx', 'gy'))
Inputs may be any that keep to these rules, and one draw needn't show every extreme that they name: `patch_of_row`: the surface nodes of one device name any one patch at most 128 times; in every draw some device names some patch exactly 128 times.
All inputs are finite; a program needn't handle non-finite values.
Results may differ from a plain program's by a relative error of at most 0.000092.
Values sent between devices are 32-bit elements; how exact they have to be, the bound alone decides.
A program may use at most 192 MiB of HBM per device.

v0:
```python
import jax
import jax.numpy as jnp
from jax import lax
from jax.sharding import PartitionSpec as P

SWEEPS = 3
NC = 64


omega_relax = 2.0 / 3.0


def with_halo(cells, sides, width):
    for axis, dim in sides:
        count = lax.axis_size(axis)
        ends = count - 1
        head = lax.slice_in_dim(cells, 0, width, axis=dim)
        tail = lax.slice_in_dim(cells, cells.shape[dim] - width, cells.shape[dim], axis=dim)
        cells = jnp.concatenate(
            [
                lax.ppermute(tail, axis, [(i, (i + 1) % count) for i in range(ends)]),
                cells,
                lax.ppermute(head, axis, [((i + 1) % count, i) for i in range(ends)]),
            ],
            axis=dim,
        )
    return cells


def six_sides(padded):
    return [
        padded[..., 2:, 1:-1, 1:-1],
        padded[..., :-2, 1:-1, 1:-1],
        padded[..., 1:-1, 2:, 1:-1],
        padded[..., 1:-1, :-2, 1:-1],
        padded[..., 1:-1, 1:-1, 2:],
        padded[..., 1:-1, 1:-1, :-2],
    ]


def pad_vertical(array):
    widths = [(0, 0)] * (array.ndim - 1) + [(1, 1)]
    return jnp.pad(array, widths)


def face_weights(center, stiff_pad):
    weights = [(center + side) * 0.5 for side in six_sides(stiff_pad)]
    diag = weights[0] + weights[1] + weights[2] + weights[3] + weights[4] + weights[5]
    return (weights, diag)


def neighbour_total(weights, scaled_pad):
    sides = six_sides(scaled_pad)
    total = weights[0][None] * sides[0]
    for index in range(1, 6):
        total = total + weights[index][None] * sides[index]
    return total


def pieces(param):
    other = 1.0 - param
    return [
        other * other * other / 6.0,
        (3.0 * param**3 - 6.0 * param * param + 4.0) / 6.0,
        (-3.0 * param**3 + 3.0 * param * param + 3.0 * param + 1.0) / 6.0,
        param**3 / 6.0,
    ]


def spline_rows(spans, param, width):
    offset = jnp.arange(width, dtype=jnp.float32)[None, None, :] - spans[:, :, None]
    basis = pieces(param)
    rows = jnp.zeros(offset.shape, jnp.float32)
    for index in range(4):
        rows = rows + jnp.where(offset == float(index), basis[index][:, :, None], 0.0)
    return rows


def contrib(floats, width):
    basis_u = spline_rows(floats[5], floats[3], width)
    basis_v = spline_rows(floats[6], floats[4], width)
    values = jnp.transpose(floats[:3], (1, 0, 2))
    left = values[:, :, :, None] * basis_u[:, None]
    return jnp.einsum(
        "pkrm,prn->pkmn",
        left,
        basis_v,
        precision=lax.Precision.HIGHEST,
        preferred_element_type=jnp.float32,
    )


def body(volume_sens, stiffness, patch_of_row, knot_spans, span_params):
    stiff_pad = pad_vertical(with_halo(stiffness, (("gx", 0), ("gy", 1)), 1))
    weights, diag = face_weights(stiffness, stiff_pad)
    field = volume_sens
    for sweep in range(SWEEPS):
        scaled = field / diag[None]
        scaled_pad = pad_vertical(with_halo(scaled, (("gx", 1), ("gy", 2)), 1))
        field = (
            volume_sens
            + (1.0 - omega_relax) * field
            + omega_relax * neighbour_total(weights, scaled_pad)
        )
    surface = omega_relax * field[:, :, :, 0] / diag[None, :, :, 0]
    row_count = surface.shape[1] * surface.shape[2]
    surface = surface.reshape(3, row_count)
    devices_all = lax.axis_size("gx") * lax.axis_size("gy")
    capacity = 4 * row_count // devices_all
    patch = patch_of_row[0, :, 0]
    one_hot = (patch[:, None] == jnp.arange(devices_all, dtype=jnp.int32)[None, :]).astype(
        jnp.int32
    )
    rank = jnp.sum(jnp.cumsum(one_hot, axis=0) * one_hot, axis=1) - 1
    slot = patch * capacity + rank
    packed = jnp.concatenate(
        [surface, span_params[0].T, knot_spans[0].T.astype(jnp.float32)], axis=0
    )
    buffer = jnp.zeros((7, devices_all * capacity), jnp.float32).at[:, slot].set(packed)
    grouped = buffer.reshape(7, devices_all, capacity)
    grads = lax.psum_scatter(contrib(grouped, NC), ("gx", "gy"), scatter_dimension=0, tiled=True)
    return (field, grads)


def solution(mesh):
    placed = (
        P(None, "gx", "gy", None),
        P("gx", "gy", None),
        P(("gx", "gy"), None, None),
        P(("gx", "gy"), None, None),
        P(("gx", "gy"), None, None),
    )
    return jax.shard_map(
        body,
        mesh=mesh,
        in_specs=placed,
        out_specs=(P(None, "gx", "gy", None), P(("gx", "gy"), None, None, None)),
        check_vma=False,
    )
```

profile of v0, /device:TPU:0, one launch (start us, length us, event | category | flops | bytes accessed | tf_op | source)
XLA Modules:
  0.0 234.0 jit_solution(17883259375930120327)
XLA Ops:
  7.9 2.3 %collective-permute-start.1 = (f32[1,32,128]{2,1,0:T(8,128)S(1)}, f32[1,32,128]{2,1,0:T(8,128)S(1)}, u32[]{:S(2)}, u32[]{:S(2)}) collective-permute-start(f32[1,32,128]{2,1,0:T(8,128)S(1)} %get-tuple-element.32), channel_id=1, source_target_pairs={{0,8},{8,16},{16,24},{1,9},{9,17},{17,25},{2,10},{10,18},{18,26},{... | collective-permute-start | bytes 49160 | tf_op jit(solution)/shard_map/ppermute | solution.py:21
  10.3 1.3 collective-permute-start
  12.7 2.8 %collective-permute-done = f32[1,32,128]{2,1,0:T(8,128)S(1)} collective-permute-done((f32[1,32,128]{2,1,0:T(8,128)S(1)}, f32[1,32,128]{2,1,0:T(8,128)S(1)}, u32[]{:S(2)}, u32[]{:S(2)}) %collective-permute-start) | collective-permute-done | bytes 16416 | tf_op jit(solution)/shard_map/ppermute | solution.py:23
  15.5 1.3 collective-permute-start.2
  16.8 4.5 %collective-permute-start.3 = (f32[34,1,128]{2,1,0:T(1,128)S(1)}, f32[34,1,128]{2,1,0:T(1,128)S(1)}, u32[]{:S(2)}, u32[]{:S(2)}) collective-permute-start(f32[34,1,128]{2,1,0:T(1,128)S(1)} %get-tuple-element.29), channel_id=1, source_target_pairs={{0,1},{1,2},{2,3},{3,4},{4,5},{5,6},{6,7},{8,9},{9,10},{10,11},{11... | collective-permute-start | bytes 52232 | tf_op jit(solution)/shard_map/ppermute | solution.py:21
  22.1 9.0 %reduce-window.6 = s32[32,8,128]{2,1,0:T(8,128)S(1)} reduce-window(s32[32,8,128]{2,1,0:T(8,128)S(1)} %fusion.83, s32[]{:T(128)} %constant.20.clone.1), window={size=1x1x128 pad=0_0x0_0x127_0}, to_apply=%region_0.1 | reduce-window | flops 4161536 | bytes 262148 | tf_op jit(solution)/shard_map/reduce-window
  33.8 1.4 collective-permute-start.4
  35.2 4.5 %collective-permute-start.5 = (f32[3,1,32,128]{3,2,1,0:T(8,128)S(1)}, f32[3,1,32,128]{3,2,1,0:T(8,128)S(1)}, u32[]{:S(2)}, u32[]{:S(2)}) collective-permute-start(f32[3,1,32,128]{3,2,1,0:T(8,128)S(1)} %get-tuple-element.27), channel_id=1, source_target_pairs={{0,8},{8,16},{16,24},{1,9},{9,17},{17,25},{2,10},{10,18},{18,26},{... | collective-permute-start | bytes 147464 | tf_op jit(solution)/shard_map/ppermute | solution.py:21
  40.6 1.3 collective-permute-start.6
  41.9 4.9 %collective-permute-start.7 = (f32[3,34,1,128]{3,2,1,0:T(1,128)S(1)}, f32[3,34,1,128]{3,2,1,0:T(1,128)S(1)}, u32[]{:S(2)}, u32[]{:S(2)}) collective-permute-start(f32[3,34,1,128]{3,2,1,0:T(1,128)S(1)} %get-tuple-element.21), channel_id=1, source_target_pairs={{0,1},{1,2},{2,3},{3,4},{4,5},{5,6},{6,7},{8,9},{9,10},{10,11},{11... | collective-permute-start | bytes 156680 | tf_op jit(solution)/shard_map/ppermute | solution.py:21
  47.0 2.1 collective-permute-done.7
  49.0 3.6 %select_maximum_fusion.8 = f32[3,34,34,130]{3,2,1,0:T(8,128)S(1)} fusion(f32[3,34,1,128]{3,2,1,0:T(1,128)S(1)} %collective-permute-done.6, f32[3,34,1,128]{3,2,1,0:T(1,128)S(1)} %collective-permute-done.7, f32[3,1,32,128]{3,2,1,0:T(8,128)S(1)} %collective-permute-done.4, f32[3,32,32,128]{3,2,1,0:T(8,128)S(1)} %broadcast_divide_fusion.2, ...), kind=kLoop, calls=%fused_computation.11 | loop fusion | flops 5410080 | bytes 3578976 | tf_op jit(solution)/shard_map/concatenate | solution.py:19
  52.6 3.0 %broadcast_divide_fusion.1 = (f32[3,32,32,128]{3,2,1,0:T(8,128)S(1)}, f32[3,32,32,128]{3,2,1,0:T(8,128)S(1)}) fusion(f32[32,32,128]{2,1,0:T(8,128)S(1)} %get-tuple-element.10, f32[3,34,34,130]{3,2,1,0:T(8,128)S(1)} %select_maximum_fusion.8, f32[32,32,128]{2,1,0:T(8,128)S(1)} %get-tuple-element.16, f32[32,32,128]{2,1,0:T(8,128)S(1)} %get-tuple-element.15, ...), kind=kLoop, calls=%fused_computation.117 | loop fusion | flops 9437184 | bytes 13309952 | tf_op jit(solution)/shard_map/div | solution.py:98
  55.6 1.3 collective-permute-start.8
  56.9 3.3 %collective-permute-start.9 = (f32[3,1,32,128]{3,2,1,0:T(8,128)S(1)}, f32[3,1,32,128]{3,2,1,0:T(8,128)S(1)}, u32[]{:S(2)}, u32[]{:S(2)}) collective-permute-start(f32[3,1,32,128]{3,2,1,0:T(8,128)S(1)} %get-tuple-element.25), channel_id=1, source_target_pairs={{0,8},{8,16},{16,24},{1,9},{9,17},{17,25},{2,10},{10,18},{18,26},{... | collective-permute-start | bytes 147464 | tf_op jit(solution)/shard_map/ppermute | solution.py:21
  61.1 1.3 collective-permute-start.10
  62.4 5.2 %collective-permute-start.11 = (f32[3,34,1,128]{3,2,1,0:T(1,128)S(1)}, f32[3,34,1,128]{3,2,1,0:T(1,128)S(1)}, u32[]{:S(2)}, u32[]{:S(2)}) collective-permute-start(f32[3,34,1,128]{3,2,1,0:T(1,128)S(1)} %get-tuple-element.19), channel_id=1, source_target_pairs={{0,1},{1,2},{2,3},{3,4},{4,5},{5,6},{6,7},{8,9},{9,10},{10,11},{11... | collective-permute-start | bytes 156680 | tf_op jit(solution)/shard_map/ppermute | solution.py:21
  67.8 1.6 collective-permute-done.11
  69.4 3.6 %select_maximum_fusion.4 = f32[3,34,34,130]{3,2,1,0:T(8,128)S(1)} fusion(f32[3,34,1,128]{3,2,1,0:T(1,128)S(1)} %collective-permute-done.10, f32[3,34,1,128]{3,2,1,0:T(1,128)S(1)} %collective-permute-done.11, f32[3,1,32,128]{3,2,1,0:T(8,128)S(1)} %collective-permute-done.8, f32[3,32,32,128]{3,2,1,0:T(8,128)S(1)} %get-tuple-element.8, ...), kind=kLoop, calls=%fused_computation.7 | loop fusion | flops 5410080 | bytes 3578976 | tf_op jit(solution)/shard_map/concatenate | solution.py:19
  73.0 4.0 %broadcast_divide_fusion = (f32[3,32,32,128]{3,2,1,0:T(8,128)S(1)}, f32[3,32,32,128]{3,2,1,0:T(8,128)}) fusion(f32[32,32,128]{2,1,0:T(8,128)S(1)} %get-tuple-element.10, f32[3,34,34,130]{3,2,1,0:T(8,128)S(1)} %select_maximum_fusion.4, f32[32,32,128]{2,1,0:T(8,128)S(1)} %get-tuple-element.16, f32[32,32,128]{2,1,0:T(8,128)S(1)} %get-tuple-element.15, ...), kind=kLoop, calls=%fused_computation.116 | loop fusion | flops 9437184 | bytes 14882816 | tf_op jit(solution)/shard_map/div | solution.py:98
  77.0 1.3 collective-permute-start.12
  78.3 5.4 %collective-permute-start.13 = (f32[3,1,32,128]{3,2,1,0:T(8,128)S(1)}, f32[3,1,32,128]{3,2,1,0:T(8,128)S(1)}, u32[]{:S(2)}, u32[]{:S(2)}) collective-permute-start(f32[3,1,32,128]{3,2,1,0:T(8,128)S(1)} %get-tuple-element.23), channel_id=1, source_target_pairs={{0,8},{8,16},{16,24},{1,9},{9,17},{17,25},{2,10},{10,18},{18,26},{... | collective-permute-start | bytes 147464 | tf_op jit(solution)/shard_map/ppermute | solution.py:21
  84.7 1.3 collective-permute-start.14
  86.0 6.0 %collective-permute-start.15 = (f32[3,34,1,128]{3,2,1,0:T(1,128)S(1)}, f32[3,34,1,128]{3,2,1,0:T(1,128)S(1)}, u32[]{:S(2)}, u32[]{:S(2)}) collective-permute-start(f32[3,34,1,128]{3,2,1,0:T(1,128)S(1)} %get-tuple-element.17), channel_id=1, source_target_pairs={{0,1},{1,2},{2,3},{3,4},{4,5},{5,6},{6,7},{8,9},{9,10},{10,11},{11... | collective-permute-start | bytes 156680 | tf_op jit(solution)/shard_map/ppermute | solution.py:21
  92.3 1.2 collective-permute-done.15
  93.5 3.6 %select_maximum_fusion = f32[3,34,34,130]{3,2,1,0:T(8,128)S(1)} fusion(f32[3,34,1,128]{3,2,1,0:T(1,128)S(1)} %collective-permute-done.14, f32[3,34,1,128]{3,2,1,0:T(1,128)S(1)} %collective-permute-done.15, f32[3,1,32,128]{3,2,1,0:T(8,128)S(1)} %collective-permute-done.12, f32[3,32,32,128]{3,2,1,0:T(8,128)S(1)} %get-tuple-element.6, ...), kind=kLoop, calls=%fused_computation.3 | loop fusion | flops 5410080 | bytes 3578976 | tf_op jit(solution)/shard_map/concatenate | solution.py:19
  97.2 2.9 %fusion.7 = f32[3,32,32,128]{3,2,1,0:T(8,128)S(1)} fusion(f32[3,34,34,130]{3,2,1,0:T(8,128)S(1)} %select_maximum_fusion, f32[3,34,1,128]{3,2,1,0:T(1,128)S(1)} %collective-permute-done.15, f32[3,1,32,128]{3,2,1,0:T(8,128)S(1)} %collective-permute-done.12, f32[3,32,32,128]{3,2,1,0:T(8,128)S(1)} %get-tuple-element.6, ...), kind=kLoop, calls=%fused_computation.31 | loop fusion | flops 9043968 | bytes 12785664 | tf_op jit(solution)/shard_map/add | solution.py:101
  100.1 1.1 copy-done.14
  102.2 3.8 %scatter_custom_fusion = f32[7,4096]{0,1:T(8,128)S(1)} fusion(s32[1024]{0:T(1024)S(1)} %bitcast.77, f32[1024,7]{1,0:T(8,128)S(1)} %copy.13, f32[]{:T(128)} %constant.17.clone.1), kind=kCustom, calls=%fused_computation.114 | custom fusion | bytes 114692 | tf_op jit(solution)/shard_map/scatter | solution.py:119
  106.0 4.4 %slice_reduce_fusion.1 = (f32[4096]{0:T(1024)S(1)}, f32[4096]{0:T(1024)S(1)}, f32[4096]{0:T(1024)S(1)}, f32[4096]{0:T(1024)S(1)}) fusion(f32[7,4096]{0,1:T(8,128)S(1)} %scatter_custom_fusion), kind=kLoop, calls=%fused_computation.20 | loop fusion | bytes 131072 | tf_op jit(solution)/shard_map/slice | solution.py:81
  111.6 4.9 %fusion.1 = f32[32,3,64,64]{3,2,1,0:T(8,128)} fusion(f32[32,128,64]{1,2,0:T(8,128)S(1)} %select_add_fusion, f32[32,3,128]{2,1,0:T(4,128)S(1)} %copy.14, f32[32,128]{1,0:T(8,128)S(1)} %get-tuple-element.42, f32[32,128]{1,0:T(8,128)S(1)} %get-tuple-element.43, f32[32,128]{1,0:T(8,128)S(1)} %get-tuple-element.41, f32[32,128]{1,0:T(8,128)S(1)} %get-tuple-element.44, ...), kind=kOutput, calls=%fused_computation.16 | convolution fusion | flops 607911936 | bytes 2752512 | tf_op jit(solution)/shard_map/pkrm,prn->pkmn/dot_general | solution.py:84
  116.5 110.7 %reduce-scatter.2.cloned.1.call-done = f32[1,3,64,64]{3,2,1,0:T(8,128)} async-done(((f32[32,3,64,64]{3,2,1,0:T(8,128)}), f32[1,3,64,64]{3,2,1,0:T(8,128)}) %reduce-scatter.2.cloned.1.call-update) | async-done | bytes 49168 | tf_op jit(solution)/shard_map/reduce_scatter | solution.py:121
  (86 shorter events, 10.6 us)
Async XLA Ops:
  7.2 220.0 %reduce-scatter.2.cloned.1.call-start = ((), (), s32[]{:S(2)}) async-start(), calls=%async_computation.1 | async-start | bytes 3244032 | tf_op jit(solution)/shard_map/reduce_scatter | solution.py:121
  7.9 3.7 %collective-permute-start.1 = (f32[1,32,128]{2,1,0:T(8,128)S(1)}, f32[1,32,128]{2,1,0:T(8,128)S(1)}, u32[]{:S(2)}, u32[]{:S(2)}) collective-permute-start(f32[1,32,128]{2,1,0:T(8,128)S(1)} %get-tuple-element.32), channel_id=1, source_target_pairs={{0,8},{8,16},{16,24},{1,9},{9,17},{17,25},{2,10},{10,18},{18,26},{... | collective-permute-start | bytes 49160 | tf_op jit(solution)/shard_map/ppermute | solution.py:21
  10.3 5.2 %collective-permute-start = (f32[1,32,128]{2,1,0:T(8,128)S(1)}, f32[1,32,128]{2,1,0:T(8,128)S(1)}, u32[]{:S(2)}, u32[]{:S(2)}) collective-permute-start(f32[1,32,128]{2,1,0:T(8,128)S(1)} %get-tuple-element.31), channel_id=1, source_target_pairs={{8,0},{16,8},{24,16},{9,1},{17,9},{25,17},{10,2},{18,10},{26,18},{... | collective-permute-start | bytes 49160 | tf_op jit(solution)/shard_map/ppermute | solution.py:23
  12.7 19.4 %copy-start.15 = (f32[32,32,128]{2,1,0:T(8,128)S(1)}, f32[32,32,128]{2,1,0:T(8,128)}, u32[]{:S(2)}) copy-start(f32[32,32,128]{2,1,0:T(8,128)} %param.6) | copy-start | bytes 1572868
  15.5 15.9 %collective-permute-start.2 = (f32[34,1,128]{2,1,0:T(1,128)S(1)}, f32[34,1,128]{2,1,0:T(1,128)S(1)}, u32[]{:S(2)}, u32[]{:S(2)}) collective-permute-start(f32[34,1,128]{2,1,0:T(1,128)S(1)} %get-tuple-element.30), channel_id=1, source_target_pairs={{1,0},{2,1},{3,2},{4,3},{5,4},{6,5},{7,6},{9,8},{10,9},{11,10},{12... | collective-permute-start | bytes 52232 | tf_op jit(solution)/shard_map/ppermute | solution.py:23
  16.8 14.6 %collective-permute-start.3 = (f32[34,1,128]{2,1,0:T(1,128)S(1)}, f32[34,1,128]{2,1,0:T(1,128)S(1)}, u32[]{:S(2)}, u32[]{:S(2)}) collective-permute-start(f32[34,1,128]{2,1,0:T(1,128)S(1)} %get-tuple-element.29), channel_id=1, source_target_pairs={{0,1},{1,2},{2,3},{3,4},{4,5},{5,6},{6,7},{8,9},{9,10},{10,11},{11... | collective-permute-start | bytes 52232 | tf_op jit(solution)/shard_map/ppermute | solution.py:21
  32.7 40.3 %copy-start.1 = (f32[32,32,128]{2,1,0:T(8,128)}, f32[32,32,128]{2,1,0:T(8,128)S(1)}, u32[]{:S(2)}) copy-start(f32[32,32,128]{2,1,0:T(8,128)S(1)} %get-tuple-element.11) | copy-start | bytes 1572868
  32.7 40.3 %copy-start.3 = (f32[32,32,128]{2,1,0:T(8,128)}, f32[32,32,128]{2,1,0:T(8,128)S(1)}, u32[]{:S(2)}) copy-start(f32[32,32,128]{2,1,0:T(8,128)S(1)} %get-tuple-element.12) | copy-start | bytes 1572868
  32.7 40.3 %copy-start.5 = (f32[32,32,128]{2,1,0:T(8,128)}, f32[32,32,128]{2,1,0:T(8,128)S(1)}, u32[]{:S(2)}) copy-start(f32[32,32,128]{2,1,0:T(8,128)S(1)} %get-tuple-element.13) | copy-start | bytes 1572868
  32.8 40.3 %copy-start.7 = (f32[32,32,128]{2,1,0:T(8,128)}, f32[32,32,128]{2,1,0:T(8,128)S(1)}, u32[]{:S(2)}) copy-start(f32[32,32,128]{2,1,0:T(8,128)S(1)} %get-tuple-element.14) | copy-start | bytes 1572868
  32.8 40.3 %copy-start.9 = (f32[32,32,128]{2,1,0:T(8,128)}, f32[32,32,128]{2,1,0:T(8,128)S(1)}, u32[]{:S(2)}) copy-start(f32[32,32,128]{2,1,0:T(8,128)S(1)} %get-tuple-element.15) | copy-start | bytes 1572868
  32.8 40.3 %copy-start.11 = (f32[32,32,128]{2,1,0:T(8,128)}, f32[32,32,128]{2,1,0:T(8,128)S(1)}, u32[]{:S(2)}) copy-start(f32[32,32,128]{2,1,0:T(8,128)S(1)} %get-tuple-element.16) | copy-start | bytes 1572868
  33.7 13.1 %copy-start.17 = (s32[1,1024,2]{1,2,0:T(2,128)S(1)}, s32[1,1024,2]{1,2,0:T(2,128)}, u32[]{:S(2)}) copy-start(s32[1,1024,2]{1,2,0:T(2,128)} %param.8) | copy-start | bytes 24580
  33.8 6.0 %collective-permute-start.4 = (f32[3,1,32,128]{3,2,1,0:T(8,128)S(1)}, f32[3,1,32,128]{3,2,1,0:T(8,128)S(1)}, u32[]{:S(2)}, u32[]{:S(2)}) collective-permute-start(f32[3,1,32,128]{3,2,1,0:T(8,128)S(1)} %get-tuple-element.28), channel_id=1, source_target_pairs={{8,0},{16,8},{24,16},{9,1},{17,9},{25,17},{10,2},{18,10},{26,18},{... | collective-permute-start | bytes 147464 | tf_op jit(solution)/shard_map/ppermute | solution.py:23
  35.2 5.3 %collective-permute-start.5 = (f32[3,1,32,128]{3,2,1,0:T(8,128)S(1)}, f32[3,1,32,128]{3,2,1,0:T(8,128)S(1)}, u32[]{:S(2)}, u32[]{:S(2)}) collective-permute-start(f32[3,1,32,128]{3,2,1,0:T(8,128)S(1)} %get-tuple-element.27), channel_id=1, source_target_pairs={{0,8},{8,16},{16,24},{1,9},{9,17},{17,25},{2,10},{10,18},{18,26},{... | collective-permute-start | bytes 147464 | tf_op jit(solution)/shard_map/ppermute | solution.py:21
  40.6 6.4 %collective-permute-start.6 = (f32[3,34,1,128]{3,2,1,0:T(1,128)S(1)}, f32[3,34,1,128]{3,2,1,0:T(1,128)S(1)}, u32[]{:S(2)}, u32[]{:S(2)}) collective-permute-start(f32[3,34,1,128]{3,2,1,0:T(1,128)S(1)} %get-tuple-element.22), channel_id=1, source_target_pairs={{1,0},{2,1},{3,2},{4,3},{5,4},{6,5},{7,6},{9,8},{10,9},{11,10},{12... | collective-permute-start | bytes 156680 | tf_op jit(solution)/shard_map/ppermute | solution.py:23
  41.9 7.1 %collective-permute-start.7 = (f32[3,34,1,128]{3,2,1,0:T(1,128)S(1)}, f32[3,34,1,128]{3,2,1,0:T(1,128)S(1)}, u32[]{:S(2)}, u32[]{:S(2)}) collective-permute-start(f32[3,34,1,128]{3,2,1,0:T(1,128)S(1)} %get-tuple-element.21), channel_id=1, source_target_pairs={{0,1},{1,2},{2,3},{3,4},{4,5},{5,6},{6,7},{8,9},{9,10},{10,11},{11... | collective-permute-start | bytes 156680 | tf_op jit(solution)/shard_map/ppermute | solution.py:21
  52.6 7.6 %copy-start.16 = (s32[1,1024,1]{1,2,0:T(1,128)S(1)}, s32[1,1024,1]{1,2,0:T(1,128)}, u32[]{:S(2)}) copy-start(s32[1,1024,1]{1,2,0:T(1,128)} %param.7) | copy-start | bytes 12292
  55.6 4.6 %collective-permute-start.8 = (f32[3,1,32,128]{3,2,1,0:T(8,128)S(1)}, f32[3,1,32,128]{3,2,1,0:T(8,128)S(1)}, u32[]{:S(2)}, u32[]{:S(2)}) collective-permute-start(f32[3,1,32,128]{3,2,1,0:T(8,128)S(1)} %get-tuple-element.26), channel_id=1, source_target_pairs={{8,0},{16,8},{24,16},{9,1},{17,9},{25,17},{10,2},{18,10},{26,18},{... | collective-permute-start | bytes 147464 | tf_op jit(solution)/shard_map/ppermute | solution.py:23
  56.9 4.1 %collective-permute-start.9 = (f32[3,1,32,128]{3,2,1,0:T(8,128)S(1)}, f32[3,1,32,128]{3,2,1,0:T(8,128)S(1)}, u32[]{:S(2)}, u32[]{:S(2)}) collective-permute-start(f32[3,1,32,128]{3,2,1,0:T(8,128)S(1)} %get-tuple-element.25), channel_id=1, source_target_pairs={{0,8},{8,16},{16,24},{1,9},{9,17},{17,25},{2,10},{10,18},{18,26},{... | collective-permute-start | bytes 147464 | tf_op jit(solution)/shard_map/ppermute | solution.py:21
  61.1 6.6 %collective-permute-start.10 = (f32[3,34,1,128]{3,2,1,0:T(1,128)S(1)}, f32[3,34,1,128]{3,2,1,0:T(1,128)S(1)}, u32[]{:S(2)}, u32[]{:S(2)}) collective-permute-start(f32[3,34,1,128]{3,2,1,0:T(1,128)S(1)} %get-tuple-element.20), channel_id=1, source_target_pairs={{1,0},{2,1},{3,2},{4,3},{5,4},{6,5},{7,6},{9,8},{10,9},{11,10},{12... | collective-permute-start | bytes 156680 | tf_op jit(solution)/shard_map/ppermute | solution.py:23
  62.4 6.9 %collective-permute-start.11 = (f32[3,34,1,128]{3,2,1,0:T(1,128)S(1)}, f32[3,34,1,128]{3,2,1,0:T(1,128)S(1)}, u32[]{:S(2)}, u32[]{:S(2)}) collective-permute-start(f32[3,34,1,128]{3,2,1,0:T(1,128)S(1)} %get-tuple-element.19), channel_id=1, source_target_pairs={{0,1},{1,2},{2,3},{3,4},{4,5},{5,6},{6,7},{8,9},{9,10},{10,11},{11... | collective-permute-start | bytes 156680 | tf_op jit(solution)/shard_map/ppermute | solution.py:21
  77.0 6.8 %collective-permute-start.12 = (f32[3,1,32,128]{3,2,1,0:T(8,128)S(1)}, f32[3,1,32,128]{3,2,1,0:T(8,128)S(1)}, u32[]{:S(2)}, u32[]{:S(2)}) collective-permute-start(f32[3,1,32,128]{3,2,1,0:T(8,128)S(1)} %get-tuple-element.24), channel_id=1, source_target_pairs={{8,0},{16,8},{24,16},{9,1},{17,9},{25,17},{10,2},{18,10},{26,18},{... | collective-permute-start | bytes 147464 | tf_op jit(solution)/shard_map/ppermute | solution.py:23
  78.3 6.3 %collective-permute-start.13 = (f32[3,1,32,128]{3,2,1,0:T(8,128)S(1)}, f32[3,1,32,128]{3,2,1,0:T(8,128)S(1)}, u32[]{:S(2)}, u32[]{:S(2)}) collective-permute-start(f32[3,1,32,128]{3,2,1,0:T(8,128)S(1)} %get-tuple-element.23), channel_id=1, source_target_pairs={{0,8},{8,16},{16,24},{1,9},{9,17},{17,25},{2,10},{10,18},{18,26},{... | collective-permute-start | bytes 147464 | tf_op jit(solution)/shard_map/ppermute | solution.py:21
  84.7 7.6 %collective-permute-start.14 = (f32[3,34,1,128]{3,2,1,0:T(1,128)S(1)}, f32[3,34,1,128]{3,2,1,0:T(1,128)S(1)}, u32[]{:S(2)}, u32[]{:S(2)}) collective-permute-start(f32[3,34,1,128]{3,2,1,0:T(1,128)S(1)} %get-tuple-element.18), channel_id=1, source_target_pairs={{1,0},{2,1},{3,2},{4,3},{5,4},{6,5},{7,6},{9,8},{10,9},{11,10},{12... | collective-permute-start | bytes 156680 | tf_op jit(solution)/shard_map/ppermute | solution.py:23
  86.0 7.5 %collective-permute-start.15 = (f32[3,34,1,128]{3,2,1,0:T(1,128)S(1)}, f32[3,34,1,128]{3,2,1,0:T(1,128)S(1)}, u32[]{:S(2)}, u32[]{:S(2)}) collective-permute-start(f32[3,34,1,128]{3,2,1,0:T(1,128)S(1)} %get-tuple-element.17), channel_id=1, source_target_pairs={{0,1},{1,2},{2,3},{3,4},{4,5},{5,6},{6,7},{8,9},{9,10},{10,11},{11... | collective-permute-start | bytes 156680 | tf_op jit(solution)/shard_map/ppermute | solution.py:21
  92.3 4.9 %copy-start.4 = (f32[32,32,128]{2,1,0:T(8,128)S(1)}, f32[32,32,128]{2,1,0:T(8,128)}, u32[]{:S(2)}) copy-start(f32[32,32,128]{2,1,0:T(8,128)} %copy-done.3) | copy-start | bytes 1572868
  92.3 4.9 %copy-start.6 = (f32[32,32,128]{2,1,0:T(8,128)S(1)}, f32[32,32,128]{2,1,0:T(8,128)}, u32[]{:S(2)}) copy-start(f32[32,32,128]{2,1,0:T(8,128)} %copy-done.5) | copy-start | bytes 1572868
  92.3 4.9 %copy-start.8 = (f32[32,32,128]{2,1,0:T(8,128)S(1)}, f32[32,32,128]{2,1,0:T(8,128)}, u32[]{:S(2)}) copy-start(f32[32,32,128]{2,1,0:T(8,128)} %copy-done.7) | copy-start | bytes 1572868
  92.3 4.9 %copy-start.10 = (f32[32,32,128]{2,1,0:T(8,128)S(1)}, f32[32,32,128]{2,1,0:T(8,128)}, u32[]{:S(2)}) copy-start(f32[32,32,128]{2,1,0:T(8,128)} %copy-done.9) | copy-start | bytes 1572868
  92.3 4.9 %copy-start.12 = (f32[32,32,128]{2,1,0:T(8,128)S(1)}, f32[32,32,128]{2,1,0:T(8,128)}, u32[]{:S(2)}) copy-start(f32[32,32,128]{2,1,0:T(8,128)} %copy-done.11) | copy-start | bytes 1572868
  92.3 4.9 %copy-start.13 = (f32[3,32,32,128]{3,2,1,0:T(8,128)S(1)}, f32[3,32,32,128]{3,2,1,0:T(8,128)}, u32[]{:S(2)}) copy-start(f32[3,32,32,128]{3,2,1,0:T(8,128)} %get-tuple-element.7) | copy-start | bytes 4718596
  (4 other events, 8.1 us)
Sparse Core Ops, SparseCore 0:
  116.6 110.4 reduce-scatter.1
where the time goes:
time: 235 us; the launch traced here: 234 us
  waiting for transfers between devices  121 us (51%)
  starting transfers between devices  46.6 us (20%)
  other arithmetic  33.1 us (14%)
  between operations  14.7 us (6%)
  local copies, waits for them, and re-layouts  13.6 us (6%)
  matrix products  4.92 us (2%)
    reduce_scatter x1, waiting for transfers between devices, body(): lax.psum_scatter(contrib(grouped, NC), ('gx', 'gy'), scatter_dimension=0,...  111 us
    ppermute x8, starting transfers between devices, with_halo(): lax.ppermute(tail, axis, [(i, (i + 1) % count) for i in range(ends)])  36.1 us
    concatenate x7, other arithmetic, with_halo(): jnp.concatenate([lax.ppermute(tail, axis, [(i, (i + 1) % count) for i in...  11.6 us
    ppermute x8, starting transfers between devices, with_halo(): lax.ppermute(head, axis, [((i + 1) % count, i) for i in range(ends)])  10.5 us
    another operation x3, other arithmetic  9.14 us
    ppermute x8, waiting for transfers between devices, with_halo(): lax.ppermute(tail, axis, [(i, (i + 1) % count) for i in range(ends)])  7.27 us
    div x3, other arithmetic, body(): scaled = field / diag[None]  7.15 us
    dot_general x1, matrix products, contrib(): jnp.einsum('pkrm,prn->pkmn', left, basis_v, precision=lax.Precision.HIGHE...  4.92 us
  transfers between devices with their start and end apart: 17, of which 10 were waited for; matrix products, arithmetic and copies ran while one was open for 5% of the time, Pallas kernels for 0%

commit v1 on v0

v1 whole, which is shorter than its diff:
```python
import functools

import jax
import jax.numpy as jnp
from jax import lax
from jax.experimental import pallas as pl
from jax.experimental.pallas import tpu as pltpu
from jax.sharding import PartitionSpec as P

SWEEPS = 3
NC = 64
OMEGA = 2.0 / 3.0
LANES = 128
EDGE = 8
MESH = pl.DeviceIdType.MESH
NT = (((1,), (1,)), ((), ()))


def pieces(param):
    other = 1.0 - param
    square = param * param
    cube = square * param
    return [
        other * other * other / 6.0,
        (3.0 * cube - 6.0 * square + 4.0) / 6.0,
        (-3.0 * cube + 3.0 * square + 3.0 * param + 1.0) / 6.0,
        cube / 6.0,
    ]


def split(values, count):
    parts = []
    for _ in range(count):
        part = values.astype(jnp.bfloat16)
        parts.append(part)
        values = values - part.astype(jnp.float32)
    return parts


def nt_dot(left, right):
    return lax.dot_general(left, right, NT, preferred_element_type=jnp.float32)


def kernel(
    sizes,
    vol_hbm, stiff_hbm, patch_ref, span_ref, param_ref,
    field_hbm, grad_ref,
    vol, cin, cpad, rd, wz, val, y0, y1, y2,
    send1, recv1, csend, crecv, send_y, recv23,
    hot_ref, slot_ref, xcol,
    meta_send, meta_recv, surf_send, surf_recv,
    bu_ref, bvh_ref, bvl_ref,
    in_sem, out_sem, ssem, rsem, cssem, crsem, mssem, mrsem, ussem, ursem,
):
    ngx, ngy, cx, cy, rows = sizes
    n = ngx * ngy
    step = cy + 2 * EDGE
    gx, gy = lax.axis_index("gx"), lax.axis_index("gy")
    me = gx * ngy + gy
    f32, bf16 = jnp.float32, jnp.bfloat16

    load_c = pltpu.make_async_copy(stiff_hbm, cin, in_sem.at[0])
    load_v = pltpu.make_async_copy(vol_hbm, vol, in_sem.at[1])
    load_c.start()
    load_v.start()

    recv1[...] = jnp.zeros(recv1.shape, f32)
    recv23[...] = jnp.zeros(recv23.shape, f32)
    crecv[...] = jnp.zeros(crecv.shape, f32)

    barrier = pltpu.get_barrier_semaphore()

    def greet(i, carry):
        to = lax.rem(me + i, n)
        pl.semaphore_signal(barrier, inc=1, device_id=(to // ngy, lax.rem(to, ngy)), device_id_type=MESH)
        return carry

    lax.fori_loop(1, n, greet, 0)

    def clear(ix, carry):
        base = pl.multiple_of(ix * step, 8)
        for y in (y1, y2):
            y[:, pl.ds(base, EDGE), :] = jnp.zeros((3, EDGE, LANES), f32)
            y[:, pl.ds(base + EDGE + cy, EDGE), :] = jnp.zeros((3, EDGE, LANES), f32)
        return carry

    lax.fori_loop(0, cx + 2, clear, 0)
    for y in (y1, y2):
        y[:, pl.ds(EDGE, cy), :] = jnp.zeros((3, cy, LANES), f32)
        y[:, pl.ds((cx + 1) * step + EDGE, cy), :] = jnp.zeros((3, cy, LANES), f32)

    sides = (
        (gx > 0, (jnp.maximum(gx - 1, 0), gy), 1),
        (gx < ngx - 1, (jnp.minimum(gx + 1, ngx - 1), gy), 0),
        (gy > 0, (gx, jnp.maximum(gy - 1, 0)), 3),
        (gy < ngy - 1, (gx, jnp.minimum(gy + 1, ngy - 1)), 2),
    )

    def face_copy(turn, side, src, dst):
        return pltpu.make_async_remote_copy(
            src_ref=src,
            dst_ref=dst.at[sides[side][2]],
            send_sem=ssem.at[turn * 4 + side],
            recv_sem=rsem.at[turn * 4 + sides[side][2]],
            device_id=sides[side][1],
            device_id_type=MESH,
        )

    def face_wait(turn, side, src, dst):
        return pltpu.make_async_remote_copy(
            src_ref=src,
            dst_ref=dst.at[side],
            send_sem=ssem.at[turn * 4 + side],
            recv_sem=rsem.at[turn * 4 + side],
            device_id=sides[side][1],
            device_id_type=MESH,
        )

    corners = []
    for a in (0, 1):
        for b in (0, 1):
            okay = jnp.logical_and(sides[a][0], sides[2 + b][0])
            corners.append((okay, (sides[a][1][0], sides[2 + b][1][1])))

    def corner_copy(index):
        return pltpu.make_async_remote_copy(
            src_ref=csend.at[index],
            dst_ref=crecv.at[3 - index],
            send_sem=cssem.at[index],
            recv_sem=crsem.at[3 - index],
            device_id=corners[index][1],
            device_id_type=MESH,
        )

    def corner_wait(index):
        return pltpu.make_async_remote_copy(
            src_ref=csend.at[index],
            dst_ref=crecv.at[index],
            send_sem=cssem.at[index],
            recv_sem=crsem.at[index],
            device_id=corners[index][1],
            device_id_type=MESH,
        )

    load_c.wait()
    load_v.wait()
    last = (cx - 1) * cy
    for k in range(3):
        send1[0, k] = vol[k, 0:cy]
        send1[1, k] = vol[k, last:last + cy]
        send1[2, k] = vol[k, pl.ds(0, cx, stride=cy)]
        send1[3, k] = vol[k, pl.ds(cy - 1, cx, stride=cy)]
    for deep in range(2):
        send1[0, 3 + deep] = cin[deep * cy:(deep + 1) * cy]
        send1[1, 3 + deep] = cin[last - deep * cy:last - deep * cy + cy]
        send1[2, 3 + deep] = cin[pl.ds(deep, cx, stride=cy)]
        send1[3, 3 + deep] = cin[pl.ds(cy - 1 - deep, cx, stride=cy)]
    for index in range(4):
        row = (index // 2) * last + (index % 2) * (cy - 1)
        csend[index] = jnp.broadcast_to(cin[row:row + 1], (8, LANES))

    pl.semaphore_wait(barrier, n - 1)
    for side in range(4):
        @pl.when(sides[side][0])
        def _(side=side):
            face_copy(0, side, send1.at[side], recv1).start()
    for index in range(4):
        @pl.when(corners[index][0])
        def _(index=index):
            corner_copy(index).start()

    patch = patch_ref[...]
    hot = (lax.broadcasted_iota(jnp.int32, (n, rows), 0) == patch).astype(f32)
    hot_ref[...] = hot
    upper = (
        lax.broadcasted_iota(jnp.int32, (LANES, LANES), 0)
        <= lax.broadcasted_iota(jnp.int32, (LANES, LANES), 1)
    ).astype(f32).astype(bf16)
    before = jnp.zeros((n, 1), f32)
    for chunk in range(rows // LANES):
        part = hot[:, chunk * LANES:(chunk + 1) * LANES]
        count = jnp.dot(part.astype(bf16), upper, preferred_element_type=f32)
        rank = jnp.sum(part * (count + before), axis=0, keepdims=True) - 1.0
        before = before + count[:, LANES - 1:LANES]
        place = lax.broadcasted_iota(jnp.int32, (LANES, LANES), 0)
        slot_ref[:, chunk * LANES:(chunk + 1) * LANES] = (
            (place == rank.astype(jnp.int32)).astype(f32).astype(bf16)
        )
    hot16 = hot.astype(bf16)
    slots = slot_ref[...]
    for q in range(2):
        total = None
        for part in split(param_ref[q:q + 1, :], 3):
            term = nt_dot(hot16 * part, slots)
            total = term if total is None else total + term
        meta_send[pl.ds(q, n, stride=8), :] = total
        knots = span_ref[q:q + 1, :].astype(f32).astype(bf16)
        meta_send[pl.ds(2 + q, n, stride=8), :] = nt_dot(hot16 * knots, slots)
    meta_send[pl.ds(4, n, stride=8), :] = jnp.zeros((n, LANES), f32)
    meta_send[pl.ds(5, n, stride=8), :] = jnp.zeros((n, LANES), f32)
    meta_send[pl.ds(6, n, stride=8), :] = jnp.zeros((n, LANES), f32)
    meta_send[pl.ds(7, n, stride=8), :] = jnp.zeros((n, LANES), f32)

    def block(number):
        return pl.ds(pl.multiple_of(number * 8, 8), 8)

    def all_copy(src, dst, sems, other, landing):
        return pltpu.make_async_remote_copy(
            src_ref=src.at[block(other)],
            dst_ref=dst.at[block(landing)],
            send_sem=sems[0].at[other],
            recv_sem=sems[1].at[landing],
            device_id=(other // ngy, lax.rem(other, ngy)),
            device_id_type=MESH,
        )

    def send_all(src, dst, sems):
        def go(i, carry):
            all_copy(src, dst, sems, lax.rem(me + i, n), me).start()
            return carry

        lax.fori_loop(1, n, go, 0)
        dst[block(me), :] = src[block(me), :]

    def take_all(src, dst, sems):
        def go(i, carry):
            other = lax.rem(me + i, n)
            all_copy(src, dst, sems, other, other).wait_recv()
            return carry

        lax.fori_loop(1, n, go, 0)

    def sent_all(src, dst, sems):
        def go(i, carry):
            all_copy(src, dst, sems, lax.rem(me + i, n), me).wait_send()
            return carry

        lax.fori_loop(1, n, go, 0)

    meta = (meta_send, meta_recv, (mssem, mrsem))
    surf = (surf_send, surf_recv, (ussem, ursem))
    send_all(*meta)

    def fill(ix, carry):
        to = pl.multiple_of((ix + 2) * step + EDGE, 8)
        cpad[pl.ds(to, cy), :] = cin[pl.ds(pl.multiple_of(ix * cy, 8), cy), :] * (OMEGA / 2)
        return carry

    lax.fori_loop(0, cx, fill, 0)
    for side in range(4):
        @pl.when(sides[side][0])
        def _(side=side):
            face_wait(0, side, send1.at[side], recv1).wait_recv()
    for index in range(4):
        @pl.when(corners[index][0])
        def _(index=index):
            corner_wait(index).wait_recv()
    half = OMEGA / 2
    for deep in range(2):
        low, high = (1 - deep) * step + EDGE, (cx + 2 + deep) * step + EDGE
        cpad[low:low + cy, :] = recv1[0, 3 + deep] * half
        cpad[high:high + cy, :] = recv1[1, 3 + deep] * half
        cpad[pl.ds(2 * step + EDGE - 1 - deep, cx, stride=step), :] = recv1[2, 3 + deep] * half
        cpad[pl.ds(2 * step + EDGE + cy + deep, cx, stride=step), :] = recv1[3, 3 + deep] * half
    for index in range(4):
        row = (1 + (index // 2) * (cx + 1)) * step + EDGE - 1 + (index % 2) * (cy + 1)
        cpad[row:row + 1, :] = crecv[index, 0:1] * half

    def inverse(center, others):
        lane = lax.broadcasted_iota(jnp.int32, center.shape, 1)
        above = jnp.where(lane == LANES - 1, 0.0, pltpu.roll(center, LANES - 1, 1))
        below = jnp.where(lane == 0, 0.0, pltpu.roll(center, 1, 1))
        total = 6.0 * center + above + below
        for other in others:
            total = total + other
        return OMEGA / total, above

    def scale(ix, carry):
        at = pl.multiple_of((ix + 2) * step + EDGE, 8)
        to = pl.multiple_of(ix * cy, 8)
        center = cpad[pl.ds(at, cy), :]
        inv, above = inverse(
            center,
            [cpad[pl.ds(at + d, cy), :] for d in (-step, step, -1, 1)],
        )
        lane = lax.broadcasted_iota(jnp.int32, center.shape, 1)
        rd[pl.ds(to, cy), :] = inv
        wz[pl.ds(to, cy), :] = jnp.where(lane == LANES - 1, 0.0, center + above)
        for k in range(3):
            y0[k, pl.ds(pl.multiple_of(at - step, 8), cy), :] = vol[k, pl.ds(to, cy), :] * inv
        return carry

    lax.fori_loop(0, cx, scale, 0)

    for side in range(4):
        if side < 2:
            at = (1 + side * (cx + 1)) * step + EDGE
            inv, _ = inverse(
                cpad[at:at + cy, :],
                [cpad[at + d:at + d + cy, :] for d in (-step, step, -1, 1)],
            )
            for k in range(3):
                y0[k, at - step + side * 0:at - step + cy, :] = recv1[side, k] * inv
        else:
            at = 2 * step + EDGE - 1 + (side - 2) * (cy + 1)
            inv, _ = inverse(
                cpad[pl.ds(at, cx, stride=step), :],
                [cpad[pl.ds(at + d, cx, stride=step), :] for d in (-step, step, -1, 1)],
            )
            for k in range(3):
                y0[k, pl.ds(at - step, cx, stride=step), :] = recv1[side, k] * inv

    def sweep(vsrc, ysrc, ydst):
        def layer(ix, carry):
            at = pl.multiple_of((ix + 1) * step + EDGE, 8)
            ct = pl.multiple_of((ix + 2) * step + EDGE, 8)
            to = pl.multiple_of(ix * cy, 8)
            center = cpad[pl.ds(ct, cy), :]
            weights = [(d, center + cpad[pl.ds(ct + d, cy), :]) for d in (step, -step, 1, -1)]
            up = wz[pl.ds(to, cy), :]
            inv = rd[pl.ds(to, cy), :]
            for k in range(3):
                mid = ysrc[k, pl.ds(at, cy), :]
                total = up * pltpu.roll(mid, LANES - 1, 1) + pltpu.roll(up * mid, 1, 1)
                for d, weight in weights:
                    total = total + weight * ysrc[k, pl.ds(at + d, cy), :]
                new = vol[k, pl.ds(to, cy), :] + (1.0 - OMEGA) * vsrc[k, pl.ds(to, cy), :] + total
                val[k, pl.ds(to, cy), :] = new
                if ydst is not None:
                    ydst[k, pl.ds(at, cy), :] = new * inv
            return carry

        lax.fori_loop(0, cx, layer, 0)

    def send_faces(turn, y):
        low, high = step + EDGE, cx * step + EDGE
        for k in range(3):
            send_y[turn - 1, 2, k] = y[k, pl.ds(low, cx, stride=step), :]
            send_y[turn - 1, 3, k] = y[k, pl.ds(low + cy - 1, cx, stride=step), :]
            send_y[turn - 1, 0, k] = y[k, low:low + cy, :]
            send_y[turn - 1, 1, k] = y[k, high:high + cy, :]
        for side in range(4):
            @pl.when(sides[side][0])
            def _(side=side):
                face_copy(turn, side, send_y.at[turn - 1, side], recv23.at[turn - 1]).start()

    def add_faces(turn, ydst):
        for side in range(4):
            @pl.when(sides[side][0])
            def _(side=side):
                face_wait(turn, side, send_y.at[turn - 1, side], recv23.at[turn - 1]).wait_recv()
        for side in range(4):
            if side < 2:
                ct = (2 + side * (cx - 1)) * step + EDGE
                to = side * last
                outer = ct + (step if side else -step)
                here, there, flat = pl.ds(ct, cy), pl.ds(outer, cy), pl.ds(to, cy)
                pad = pl.ds(ct - step, cy)
            else:
                shift = (side - 2) * (cy - 1)
                ct = 2 * step + EDGE + shift
                outer = ct + (1 if side == 3 else -1)
                here, there = pl.ds(ct, cx, stride=step), pl.ds(outer, cx, stride=step)
                flat = pl.ds(shift, cx, stride=cy)
                pad = pl.ds(ct - step, cx, stride=step)
            weight = cpad[here, :] + cpad[there, :]
            inv = rd[flat, :]
            for k in range(3):
                more = weight * recv23[turn - 1, side, k]
                val[k, flat, :] = val[k, flat, :] + more
                if ydst is not None:
                    ydst[k, pad, :] = ydst[k, pad, :] + more * inv

    sweep(vol, y0, y1)
    send_faces(1, y1)
    sweep(val, y1, y2)
    add_faces(1, y2)
    send_faces(2, y2)
    sweep(val, y2, None)

    take_all(*meta)
    basis_u = pieces(meta_recv[pl.ds(0, n, stride=8), :])
    basis_v = pieces(meta_recv[pl.ds(1, n, stride=8), :])
    span_u = meta_recv[pl.ds(2, n, stride=8), :].astype(jnp.int32)
    span_v = meta_recv[pl.ds(3, n, stride=8), :].astype(jnp.int32)
    knot = lax.broadcasted_iota(jnp.int32, (NC, LANES), 0)

    def spline(span, basis, d):
        offset = knot - span[d:d + 1, :]
        out = jnp.where(offset == 0, basis[0][d:d + 1, :], 0.0)
        for index in range(1, 4):
            out = jnp.where(offset == index, basis[index][d:d + 1, :], out)
        return out

    for d in range(n):
        lanes = slice(d * LANES, (d + 1) * LANES)
        bu_ref[:, lanes] = spline(span_u, basis_u, d)
        high, low = split(spline(span_v, basis_v, d), 2)
        bvh_ref[:, lanes] = high
        bvl_ref[:, lanes] = low

    add_faces(2, None)
    store = pltpu.make_async_copy(val, field_hbm, out_sem)
    store.start()

    def surface(ix, carry):
        to = pl.ds(pl.multiple_of(ix * cy, 8), cy)
        lane = lax.broadcasted_iota(jnp.int32, (cy, LANES), 1)
        inv = rd[to, :] * OMEGA
        out = jnp.where(lane == 0, val[0, to, :] * inv, 0.0)
        for k in (1, 2):
            out = jnp.where(lane == k, pltpu.roll(val[k, to, :] * inv, k, 1), out)
        xcol[to, :] = out
        return carry

    lax.fori_loop(0, cx, surface, 0)
    surf_rows = jnp.concatenate(
        [xcol[c * LANES:(c + 1) * LANES, :].T[0:8] for c in range(rows // LANES)], axis=1
    )
    hot16 = hot_ref[...].astype(bf16)
    slots = slot_ref[...]
    for k in range(3):
        total = None
        for part in split(surf_rows[k:k + 1, :], 3):
            term = nt_dot(hot16 * part, slots)
            total = term if total is None else total + term
        surf_send[pl.ds(k, n, stride=8), :] = total
    for k in range(3, 8):
        surf_send[pl.ds(k, n, stride=8), :] = jnp.zeros((n, LANES), f32)
    send_all(*surf)
    take_all(*surf)

    group = 8
    total = jnp.zeros((3 * NC, NC), f32)
    for first in range(0, n, group):
        lanes = slice(first * LANES, (first + group) * LANES)
        bu = bu_ref[:, lanes]
        left = jnp.concatenate(
            [
                bu * jnp.concatenate(
                    [surf_recv[d * 8 + k:d * 8 + k + 1, :] for d in range(first, first + group)],
                    axis=1,
                )
                for k in range(3)
            ],
            axis=0,
        )
        high, low = split(left, 2)
        bvh = bvh_ref[:, lanes]
        total = total + nt_dot(high, bvh) + nt_dot(low, bvh) + nt_dot(high, bvl_ref[:, lanes])
    for k in range(3):
        grad_ref[k] = total[k * NC:(k + 1) * NC]

    for side in range(4):
        @pl.when(sides[side][0])
        def _(side=side):
            face_copy(0, side, send1.at[side], recv1).wait_send()
            for turn in (1, 2):
                face_copy(turn, side, send_y.at[turn - 1, side], recv23.at[turn - 1]).wait_send()
    for index in range(4):
        @pl.when(corners[index][0])
        def _(index=index):
            corner_copy(index).wait_send()
    sent_all(*meta)
    sent_all(*surf)
    store.wait()


def body(volume_sens, stiffness, patch_of_row, knot_spans, span_params):
    ngx, ngy = lax.axis_size("gx"), lax.axis_size("gy")
    n = ngx * ngy
    _, cx, cy, nz = volume_sens.shape
    rows = cx * cy
    step = cy + 2 * EDGE
    f32, bf16 = jnp.float32, jnp.bfloat16
    dma = pltpu.SemaphoreType.DMA
    field, grads = pl.pallas_call(
        functools.partial(kernel, (ngx, ngy, cx, cy, rows)),
        out_shape=(
            jax.ShapeDtypeStruct((3, rows, nz), f32),
            jax.ShapeDtypeStruct((3, NC, NC), f32),
        ),
        in_specs=[
            pl.BlockSpec(memory_space=pl.ANY),
            pl.BlockSpec(memory_space=pl.ANY),
            pl.BlockSpec(memory_space=pltpu.VMEM),
            pl.BlockSpec(memory_space=pltpu.VMEM),
            pl.BlockSpec(memory_space=pltpu.VMEM),
        ],
        out_specs=(
            pl.BlockSpec(memory_space=pl.ANY),
            pl.BlockSpec(memory_space=pltpu.VMEM),
        ),
        scratch_shapes=[
            pltpu.VMEM((3, rows, nz), f32),
            pltpu.VMEM((rows, nz), f32),
            pltpu.VMEM(((cx + 4) * step, nz), f32),
            pltpu.VMEM((rows, nz), f32),
            pltpu.VMEM((rows, nz), f32),
            pltpu.VMEM((3, rows, nz), f32),
            pltpu.VMEM((3, (cx + 2) * step, nz), f32),
            pltpu.VMEM((3, (cx + 2) * step, nz), f32),
            pltpu.VMEM((3, (cx + 2) * step, nz), f32),
            pltpu.VMEM((4, 5, cy, nz), f32),
            pltpu.VMEM((4, 5, cy, nz), f32),
            pltpu.VMEM((4, 8, nz), f32),
            pltpu.VMEM((4, 8, nz), f32),
            pltpu.VMEM((2, 4, 3, cy, nz), f32),
            pltpu.VMEM((2, 4, 3, cy, nz), f32),
            pltpu.VMEM((n, rows), f32),
            pltpu.VMEM((LANES, rows), bf16),
            pltpu.VMEM((rows, nz), f32),
            pltpu.VMEM((n * 8, LANES), f32),
            pltpu.VMEM((n * 8, LANES), f32),
            pltpu.VMEM((n * 8, LANES), f32),
            pltpu.VMEM((n * 8, LANES), f32),
            pltpu.VMEM((NC, n * LANES), f32),
            pltpu.VMEM((NC, n * LANES), bf16),
            pltpu.VMEM((NC, n * LANES), bf16),
            dma((2,)),
            dma,
            dma((12,)),
            dma((12,)),
            dma((4,)),
            dma((4,)),
            dma((n,)),
            dma((n,)),
            dma((n,)),
            dma((n,)),
        ],
        compiler_params=pltpu.CompilerParams(
            collective_id=0, has_side_effects=True, vmem_limit_bytes=56 * 2**20
        ),
    )(
        volume_sens.reshape(3, rows, nz),
        stiffness.reshape(rows, nz),
        patch_of_row.reshape(1, rows),
        knot_spans[0].T,
        span_params[0].T,
    )
    return field.reshape(volume_sens.shape), grads[None]


def solution(mesh):
    placed = (
        P(None, "gx", "gy", None),
        P("gx", "gy", None),
        P(("gx", "gy"), None, None),
        P(("gx", "gy"), None, None),
        P(("gx", "gy"), None, None),
    )
    return jax.shard_map(
        body,
        mesh=mesh,
        in_specs=placed,
        out_specs=(P(None, "gx", "gy", None), P(("gx", "gy"), None, None, None)),
        check_vma=False,
    )
```

time: 235 us -> 46.3 us (0.20)
  waiting for transfers between devices: 121 us -> 0 us
  starting transfers between devices: 46.6 us -> 0 us
  Pallas kernels: 0 us -> 42 us
  other arithmetic: 33.1 us -> 0 us
  between operations: 14.7 us -> 0.65 us
  local copies, waits for them, and re-layouts: 13.6 us -> 3.35 us
  matrix products: 4.92 us -> 0 us
    reduce_scatter x1 -> x0, waiting for transfers between devices: 111 us -> none  [body(): lax.psum_scatter(contrib(grouped, NC), ('gx', 'gy'), scatter_dimension=0,...]
    ppermute x16 -> x0, starting transfers between devices: 46.6 us -> none  [the longest x8 36.1 us: with_halo(): lax.ppermute(tail, axis, [(i, (i + 1) % count) for i in range(ends)])]
    pallas_call x0 -> x1, Pallas kernels: none -> 42 us  [body(): pl.pallas_call(functools.partial(kernel, (ngx, ngy, cx, cy, rows)), out_s...]
    concatenate x8 -> x0, other arithmetic: 11.6 us -> none  [the longest x7 11.6 us: with_halo(): jnp.concatenate([lax.ppermute(tail, axis, [(i, (i + 1) % count) for i in...]
    ppermute x16 -> x0, waiting for transfers between devices: 10.4 us -> none  [the longest x8 7.27 us: with_halo(): lax.ppermute(tail, axis, [(i, (i + 1) % count) for i in range(ends)])]
    another operation x3 -> x0, other arithmetic: 9.14 us -> none
    div x5 -> x0, other arithmetic: 7.2 us -> none  [the longest x3 7.15 us: body(): scaled = field / diag[None]]
    slice x9 -> x0, local copies, waits for them, and re-layouts: 5.62 us -> none  [the longest x1 4.41 us: contrib(): basis_v = spline_rows(floats[6], floats[4], width)]
  transfers between devices with their start and end apart: 17 -> 0, of which waited for: 10 -> 0; matrix products, arithmetic and copies ran while one was open for 5% -> 0% of each run, Pallas kernels for 0% -> 0%
where the time goes in v1:
time: 46.3 us; the launch traced here: 46 us
  Pallas kernels  42 us (91%)
  local copies, waits for them, and re-layouts  3.35 us (7%)
  between operations  0.65 us (1%)
    pallas_call x1, Pallas kernels, body(): pl.pallas_call(functools.partial(kernel, (ngx, ngy, cx, cy, rows)), out_s...  42 us
    unnamed x4, local copies, waits for them, and re-layouts  3.35 us

profile of v1, /device:TPU:0, one launch (start us, length us, event | category | flops | bytes accessed | tf_op | source)
XLA Modules:
  0.0 46.0 jit_solution(17559653970062122034)
XLA Ops:
  0.6 42.0 %shard_map.68 = (f32[3,1024,128]{2,1,0:T(8,128)}, f32[3,64,64]{2,1,0:T(8,128)}) custom-call(f32[3,1024,128]{2,1,0:T(8,128)} %bitcast.12, f32[1024,128]{1,0:T(8,128)} %bitcast.13, s32[1,1024]{1,0:T(1,128)} %bitcast.17, s32[2,1024]{1,0:T(2,128)} %bitcast.15, f32[2,1024]{1,0:T(2,128)} %bitcast.16), custom_call_target="tpu_custom_call" | custom-call | tf_op jit(solution)/shard_map/pallas_call | solution.py:477
  42.7 0.0 copy-start
  42.7 2.7 %copy.9 = f32[3,32,32,128]{3,2,1,0:T(8,128)} copy(f32[3,32,32,128]{3,2,1,0:T(8,128)} %bitcast.11) | data formatting | bytes 3145728
  45.4 0.0 copy-done
  45.4 0.6 %copy.10 = f32[1,3,64,64]{3,2,1,0:T(8,128)} copy(f32[1,3,64,64]{3,2,1,0:T(8,128)S(1)} %bitcast.14) | data formatting | bytes 98304
Async XLA Ops:
  42.7 2.7 %copy-start = (f32[3,64,64]{2,1,0:T(8,128)S(1)}, f32[3,64,64]{2,1,0:T(8,128)}, u32[]{:S(2)}) copy-start(f32[3,64,64]{2,1,0:T(8,128)} %get-tuple-element.5) | copy-start | bytes 147460

commit v2 on v1

--- a/solution.py
+++ b/solution.py
@@ -12,6 +12,7 @@
 OMEGA = 2.0 / 3.0
 LANES = 128
 EDGE = 8
+UNROLL = 4
 MESH = pl.DeviceIdType.MESH
 NT = (((1,), (1,)), ((), ()))
 
@@ -44,13 +45,13 @@
 def kernel(
     sizes,
     vol_hbm, stiff_hbm, patch_ref, span_ref, param_ref,
-    field_hbm, grad_ref,
+    field, grad_ref,
     vol, cin, cpad, rd, wz, val, y0, y1, y2,
     send1, recv1, csend, crecv, send_y, recv23,
     hot_ref, slot_ref, xcol,
     meta_send, meta_recv, surf_send, surf_recv,
-    bu_ref, bvh_ref, bvl_ref,
-    in_sem, out_sem, ssem, rsem, cssem, crsem, mssem, mrsem, ussem, ursem,
+    bu_ref, bv_ref,
+    in_sem, ssem, rsem, cssem, crsem, mssem, mrsem, ussem, ursem,
 ):
     ngx, ngy, cx, cy, rows = sizes
     n = ngx * ngy
@@ -188,14 +189,17 @@
         )
     hot16 = hot.astype(bf16)
     slots = slot_ref[...]
+    stack = []
     for q in range(2):
-        total = None
-        for part in split(param_ref[q:q + 1, :], 3):
-            term = nt_dot(hot16 * part, slots)
-            total = term if total is None else total + term
-        meta_send[pl.ds(q, n, stride=8), :] = total
-        knots = span_ref[q:q + 1, :].astype(f32).astype(bf16)
-        meta_send[pl.ds(2 + q, n, stride=8), :] = nt_dot(hot16 * knots, slots)
+        stack += split(param_ref[q:q + 1, :], 3)
+    for q in range(2):
+        stack.append(span_ref[q:q + 1, :].astype(f32).astype(bf16))
+    out = nt_dot(jnp.concatenate([hot16 * part for part in stack], axis=0), slots)
+    out = [out[i * n:(i + 1) * n] for i in range(8)]
+    meta_send[pl.ds(0, n, stride=8), :] = out[0] + out[1] + out[2]
+    meta_send[pl.ds(1, n, stride=8), :] = out[3] + out[4] + out[5]
+    meta_send[pl.ds(2, n, stride=8), :] = out[6]
+    meta_send[pl.ds(3, n, stride=8), :] = out[7]
     meta_send[pl.ds(4, n, stride=8), :] = jnp.zeros((n, LANES), f32)
     meta_send[pl.ds(5, n, stride=8), :] = jnp.zeros((n, LANES), f32)
     meta_send[pl.ds(6, n, stride=8), :] = jnp.zeros((n, LANES), f32)
@@ -246,7 +250,7 @@
         cpad[pl.ds(to, cy), :] = cin[pl.ds(pl.multiple_of(ix * cy, 8), cy), :] * (OMEGA / 2)
         return carry
 
-    lax.fori_loop(0, cx, fill, 0)
+    lax.fori_loop(0, cx, fill, 0, unroll=UNROLL)
     for side in range(4):
         @pl.when(sides[side][0])
         def _(side=side):
@@ -275,22 +279,27 @@
             total = total + other
         return OMEGA / total, above
 
-    def scale(ix, carry):
-        at = pl.multiple_of((ix + 2) * step + EDGE, 8)
-        to = pl.multiple_of(ix * cy, 8)
-        center = cpad[pl.ds(at, cy), :]
-        inv, above = inverse(
-            center,
-            [cpad[pl.ds(at + d, cy), :] for d in (-step, step, -1, 1)],
-        )
-        lane = lax.broadcasted_iota(jnp.int32, center.shape, 1)
-        rd[pl.ds(to, cy), :] = inv
-        wz[pl.ds(to, cy), :] = jnp.where(lane == LANES - 1, 0.0, center + above)
-        for k in range(3):
-            y0[k, pl.ds(pl.multiple_of(at - step, 8), cy), :] = vol[k, pl.ds(to, cy), :] * inv
+    def scale(it, carry):
+        done = []
+        for u in range(UNROLL):
+            ix = it * UNROLL + u
+            at = pl.multiple_of((ix + 2) * step + EDGE, 8)
+            to = pl.multiple_of(ix * cy, 8)
+            center = cpad[pl.ds(at, cy), :]
+            inv, above = inverse(
+                center,
+                [cpad[pl.ds(at + d, cy), :] for d in (-step, step, -1, 1)],
+            )
+            lane = lax.broadcasted_iota(jnp.int32, center.shape, 1)
+            up = jnp.where(lane == LANES - 1, 0.0, center + above)
+            done.append((at, to, inv, up, vol[:, pl.ds(to, cy), :] * inv[None]))
+        for at, to, inv, up, scaled in done:
+            rd[pl.ds(to, cy), :] = inv
+            wz[pl.ds(to, cy), :] = up
+            y0[:, pl.ds(pl.multiple_of(at - step, 8), cy), :] = scaled
         return carry
 
-    lax.fori_loop(0, cx, scale, 0)
+    lax.fori_loop(0, cx // UNROLL, scale, 0)
 
     for side in range(4):
         if side < 2:
@@ -310,27 +319,30 @@
             for k in range(3):
                 y0[k, pl.ds(at - step, cx, stride=step), :] = recv1[side, k] * inv
 
-    def sweep(vsrc, ysrc, ydst):
-        def layer(ix, carry):
-            at = pl.multiple_of((ix + 1) * step + EDGE, 8)
-            ct = pl.multiple_of((ix + 2) * step + EDGE, 8)
-            to = pl.multiple_of(ix * cy, 8)
-            center = cpad[pl.ds(ct, cy), :]
-            weights = [(d, center + cpad[pl.ds(ct + d, cy), :]) for d in (step, -step, 1, -1)]
-            up = wz[pl.ds(to, cy), :]
-            inv = rd[pl.ds(to, cy), :]
-            for k in range(3):
-                mid = ysrc[k, pl.ds(at, cy), :]
-                total = up * pltpu.roll(mid, LANES - 1, 1) + pltpu.roll(up * mid, 1, 1)
-                for d, weight in weights:
-                    total = total + weight * ysrc[k, pl.ds(at + d, cy), :]
-                new = vol[k, pl.ds(to, cy), :] + (1.0 - OMEGA) * vsrc[k, pl.ds(to, cy), :] + total
-                val[k, pl.ds(to, cy), :] = new
+    def sweep(vsrc, vdst, ysrc, ydst):
+        def layers(it, carry):
+            done = []
+            for u in range(UNROLL):
+                ix = it * UNROLL + u
+                at = pl.multiple_of((ix + 1) * step + EDGE, 8)
+                ct = pl.multiple_of((ix + 2) * step + EDGE, 8)
+                to = pl.multiple_of(ix * cy, 8)
+                center = cpad[pl.ds(ct, cy), :]
+                up = wz[pl.ds(to, cy), :][None]
+                mid = ysrc[:, pl.ds(at, cy), :]
+                total = up * pltpu.roll(mid, LANES - 1, 2) + pltpu.roll(up * mid, 1, 2)
+                for d in (step, -step, 1, -1):
+                    weight = center + cpad[pl.ds(ct + d, cy), :]
+                    total = total + weight[None] * ysrc[:, pl.ds(at + d, cy), :]
+                new = vol[:, pl.ds(to, cy), :] + (1.0 - OMEGA) * vsrc[:, pl.ds(to, cy), :] + total
+                done.append((at, to, new))
+            for at, to, new in done:
+                vdst[:, pl.ds(to, cy), :] = new
                 if ydst is not None:
-                    ydst[k, pl.ds(at, cy), :] = new * inv
+                    ydst[:, pl.ds(at, cy), :] = new * rd[pl.ds(to, cy), :][None]
             return carry
 
-        lax.fori_loop(0, cx, layer, 0)
+        lax.fori_loop(0, cx // UNROLL, layers, 0)
 
     def send_faces(turn, y):
         low, high = step + EDGE, cx * step + EDGE
@@ -344,7 +356,7 @@
             def _(side=side):
                 face_copy(turn, side, send_y.at[turn - 1, side], recv23.at[turn - 1]).start()
 
-    def add_faces(turn, ydst):
+    def add_faces(turn, val, ydst):
         for side in range(4):
             @pl.when(sides[side][0])
             def _(side=side):
@@ -371,12 +383,12 @@
                 if ydst is not None:
                     ydst[k, pad, :] = ydst[k, pad, :] + more * inv
 
-    sweep(vol, y0, y1)
+    sweep(vol, field, y0, y1)
     send_faces(1, y1)
-    sweep(val, y1, y2)
-    add_faces(1, y2)
+    sweep(field, val, y1, y2)
+    add_faces(1, val, y2)
     send_faces(2, y2)
-    sweep(val, y2, None)
+    sweep(val, field, y2, None)
 
     take_all(*meta)
     basis_u = pieces(meta_recv[pl.ds(0, n, stride=8), :])
@@ -396,42 +408,41 @@
         lanes = slice(d * LANES, (d + 1) * LANES)
         bu_ref[:, lanes] = spline(span_u, basis_u, d)
         high, low = split(spline(span_v, basis_v, d), 2)
-        bvh_ref[:, lanes] = high
-        bvl_ref[:, lanes] = low
-
-    add_faces(2, None)
-    store = pltpu.make_async_copy(val, field_hbm, out_sem)
-    store.start()
+        bv_ref[:NC, lanes] = high
+        bv_ref[NC:, lanes] = low
+
+    add_faces(2, field, None)
 
     def surface(ix, carry):
         to = pl.ds(pl.multiple_of(ix * cy, 8), cy)
         lane = lax.broadcasted_iota(jnp.int32, (cy, LANES), 1)
         inv = rd[to, :] * OMEGA
-        out = jnp.where(lane == 0, val[0, to, :] * inv, 0.0)
+        out = jnp.where(lane == 0, field[0, to, :] * inv, 0.0)
         for k in (1, 2):
-            out = jnp.where(lane == k, pltpu.roll(val[k, to, :] * inv, k, 1), out)
+            out = jnp.where(lane == k, pltpu.roll(field[k, to, :] * inv, k, 1), out)
         xcol[to, :] = out
         return carry
 
-    lax.fori_loop(0, cx, surface, 0)
+    lax.fori_loop(0, cx, surface, 0, unroll=UNROLL)
     surf_rows = jnp.concatenate(
         [xcol[c * LANES:(c + 1) * LANES, :].T[0:8] for c in range(rows // LANES)], axis=1
     )
     hot16 = hot_ref[...].astype(bf16)
     slots = slot_ref[...]
+    stack = []
     for k in range(3):
-        total = None
-        for part in split(surf_rows[k:k + 1, :], 3):
-            term = nt_dot(hot16 * part, slots)
-            total = term if total is None else total + term
-        surf_send[pl.ds(k, n, stride=8), :] = total
+        stack += split(surf_rows[k:k + 1, :], 3)
+    out = nt_dot(jnp.concatenate([hot16 * part for part in stack], axis=0), slots)
+    out = [out[i * n:(i + 1) * n] for i in range(9)]
+    for k in range(3):
+        surf_send[pl.ds(k, n, stride=8), :] = out[3 * k] + out[3 * k + 1] + out[3 * k + 2]
     for k in range(3, 8):
         surf_send[pl.ds(k, n, stride=8), :] = jnp.zeros((n, LANES), f32)
     send_all(*surf)
     take_all(*surf)
 
     group = 8
-    total = jnp.zeros((3 * NC, NC), f32)
+    total = jnp.zeros((6 * NC, 2 * NC), f32)
     for first in range(0, n, group):
         lanes = slice(first * LANES, (first + group) * LANES)
         bu = bu_ref[:, lanes]
@@ -445,11 +456,10 @@
             ],
             axis=0,
         )
-        high, low = split(left, 2)
-        bvh = bvh_ref[:, lanes]
-        total = total + nt_dot(high, bvh) + nt_dot(low, bvh) + nt_dot(high, bvl_ref[:, lanes])
+        total = total + nt_dot(jnp.concatenate(split(left, 2), axis=0), bv_ref[:, lanes])
     for k in range(3):
-        grad_ref[k] = total[k * NC:(k + 1) * NC]
+        high, low = total[k * NC:(k + 1) * NC], total[(3 + k) * NC:(4 + k) * NC]
+        grad_ref[k] = high[:, :NC] + high[:, NC:] + low[:, :NC] + low[:, NC:]
 
     for side in range(4):
         @pl.when(sides[side][0])
@@ -463,7 +473,6 @@
             corner_copy(index).wait_send()
     sent_all(*meta)
     sent_all(*surf)
-    store.wait()
 
 
 def body(volume_sens, stiffness, patch_of_row, knot_spans, span_params):
@@ -477,8 +486,8 @@
     field, grads = pl.pallas_call(
         functools.partial(kernel, (ngx, ngy, cx, cy, rows)),
         out_shape=(
-            jax.ShapeDtypeStruct((3, rows, nz), f32),
-            jax.ShapeDtypeStruct((3, NC, NC), f32),
+            pltpu.VMEM((3, rows, nz), f32),
+            pltpu.VMEM((3, NC, NC), f32),
         ),
         in_specs=[
             pl.BlockSpec(memory_space=pl.ANY),
@@ -488,7 +497,7 @@
             pl.BlockSpec(memory_space=pltpu.VMEM),
         ],
         out_specs=(
-            pl.BlockSpec(memory_space=pl.ANY),
+            pl.BlockSpec(memory_space=pltpu.VMEM),
             pl.BlockSpec(memory_space=pltpu.VMEM),
         ),
         scratch_shapes=[
@@ -515,10 +524,8 @@
             pltpu.VMEM((n * 8, LANES), f32),
             pltpu.VMEM((n * 8, LANES), f32),
             pltpu.VMEM((NC, n * LANES), f32),
-            pltpu.VMEM((NC, n * LANES), bf16),
-            pltpu.VMEM((NC, n * LANES), bf16),
+            pltpu.VMEM((2 * NC, n * LANES), bf16),
             dma((2,)),
-            dma,
             dma((12,)),
             dma((12,)),
             dma((4,)),

time: 46.3 us -> 37.1 us (0.80)
  Pallas kernels: 42 us -> 34.4 us
  local copies, waits for them, and re-layouts: 3.35 us -> 1.79 us
    pallas_call x1, Pallas kernels: 42 us -> 34.4 us  [body(): pl.pallas_call(functools.partial(kernel, (ngx, ngy, cx, cy, rows)), out_s...]
    unnamed x4 -> x2, local copies, waits for them, and re-layouts: 3.35 us -> 1.79 us
where the time goes in v2:
time: 37.1 us; the launch traced here: 36.8 us
  Pallas kernels  34.4 us (93%)
  local copies, waits for them, and re-layouts  1.79 us (5%)
  between operations  0.64 us (2%)
    pallas_call x1, Pallas kernels, body(): pl.pallas_call(functools.partial(kernel, (ngx, ngy, cx, cy, rows)), out_s...  34.4 us
    unnamed x2, local copies, waits for them, and re-layouts  1.79 us

profile of v2, /device:TPU:0, one launch (start us, length us, event | category | flops | bytes accessed | tf_op | source)
XLA Modules:
  0.0 36.8 jit_solution(3541953903493078406)
XLA Ops:
  0.6 34.4 %shard_map.68 = (f32[3,1024,128]{2,1,0:T(8,128)S(1)}, f32[3,64,64]{2,1,0:T(8,128)S(1)}) custom-call(f32[3,1024,128]{2,1,0:T(8,128)} %bitcast.13, f32[1024,128]{1,0:T(8,128)} %bitcast.14, s32[1,1024]{1,0:T(1,128)} %bitcast.17, s32[2,1024]{1,0:T(2,128)} %bitcast.15, f32[2,1024]{1,0:T(2,128)} %bitcast.16), custom_call_target="tpu_custom_call" | custom-call | tf_op jit(solution)/shard_map/pallas_call | solution.py:486
  35.0 1.1 %copy.9 = f32[3,32,32,128]{3,2,1,0:T(8,128)} copy(f32[3,32,32,128]{3,2,1,0:T(8,128)S(1)} %bitcast.11) | data formatting | bytes 3145728
  36.2 0.6 %copy.10 = f32[1,3,64,64]{3,2,1,0:T(8,128)} copy(f32[1,3,64,64]{3,2,1,0:T(8,128)S(1)} %bitcast.12) | data formatting | bytes 98304

commit v3 on v2

--- a/solution.py
+++ b/solution.py
@@ -45,12 +45,11 @@
 def kernel(
     sizes,
     vol_hbm, stiff_hbm, patch_ref, span_ref, param_ref,
-    field, grad_ref,
+    field, surf_recv, bu_ref, bv_ref,
     vol, cin, cpad, rd, wz, val, y0, y1, y2,
     send1, recv1, csend, crecv, send_y, recv23,
     hot_ref, slot_ref, xcol,
-    meta_send, meta_recv, surf_send, surf_recv,
-    bu_ref, bv_ref,
+    meta_send, meta_recv, surf_send,
     in_sem, ssem, rsem, cssem, crsem, mssem, mrsem, ussem, ursem,
 ):
     ngx, ngy, cx, cy, rows = sizes
@@ -65,10 +64,6 @@
     load_c.start()
     load_v.start()
 
-    recv1[...] = jnp.zeros(recv1.shape, f32)
-    recv23[...] = jnp.zeros(recv23.shape, f32)
-    crecv[...] = jnp.zeros(crecv.shape, f32)
-
     barrier = pltpu.get_barrier_semaphore()
 
     def greet(i, carry):
@@ -77,18 +72,6 @@
         return carry
 
     lax.fori_loop(1, n, greet, 0)
-
-    def clear(ix, carry):
-        base = pl.multiple_of(ix * step, 8)
-        for y in (y1, y2):
-            y[:, pl.ds(base, EDGE), :] = jnp.zeros((3, EDGE, LANES), f32)
-            y[:, pl.ds(base + EDGE + cy, EDGE), :] = jnp.zeros((3, EDGE, LANES), f32)
-        return carry
-
-    lax.fori_loop(0, cx + 2, clear, 0)
-    for y in (y1, y2):
-        y[:, pl.ds(EDGE, cy), :] = jnp.zeros((3, cy, LANES), f32)
-        y[:, pl.ds((cx + 1) * step + EDGE, cy), :] = jnp.zeros((3, cy, LANES), f32)
 
     sides = (
         (gx > 0, (jnp.maximum(gx - 1, 0), gy), 1),
@@ -142,6 +125,33 @@
             device_id=corners[index][1],
             device_id_type=MESH,
         )
+
+    for side in range(4):
+        @pl.when(jnp.logical_not(sides[side][0]))
+        def _(side=side):
+            recv1[side] = jnp.zeros(recv1.shape[1:], f32)
+            for turn in range(2):
+                recv23[turn, side] = jnp.zeros(recv23.shape[2:], f32)
+    for index in range(4):
+        @pl.when(jnp.logical_not(corners[index][0]))
+        def _(index=index):
+            crecv[index] = jnp.zeros(crecv.shape[1:], f32)
+
+    def clear(ix, carry):
+        base = pl.multiple_of(ix * step, 8)
+        for y in (y0, y1, y2):
+            y[:, pl.ds(base, EDGE), :] = jnp.zeros((3, EDGE, LANES), f32)
+            y[:, pl.ds(base + EDGE + cy, EDGE), :] = jnp.zeros((3, EDGE, LANES), f32)
+        cpad[pl.ds(base + step, EDGE), :] = jnp.zeros((EDGE, LANES), f32)
+        cpad[pl.ds(base + step + EDGE + cy, EDGE), :] = jnp.zeros((EDGE, LANES), f32)
+        return carry
+
+    lax.fori_loop(0, cx + 2, clear, 0)
+    for y in (y0, y1, y2):
+        y[:, pl.ds(EDGE, cy), :] = jnp.zeros((3, cy, LANES), f32)
+        y[:, pl.ds((cx + 1) * step + EDGE, cy), :] = jnp.zeros((3, cy, LANES), f32)
+    for layer in (0, 1, cx + 2, cx + 3):
+        cpad[pl.ds(layer * step + EDGE, cy), :] = jnp.zeros((cy, LANES), f32)
 
     load_c.wait()
     load_v.wait()
@@ -170,48 +180,10 @@
         def _(index=index):
             corner_copy(index).start()
 
-    patch = patch_ref[...]
-    hot = (lax.broadcasted_iota(jnp.int32, (n, rows), 0) == patch).astype(f32)
-    hot_ref[...] = hot
-    upper = (
-        lax.broadcasted_iota(jnp.int32, (LANES, LANES), 0)
-        <= lax.broadcasted_iota(jnp.int32, (LANES, LANES), 1)
-    ).astype(f32).astype(bf16)
-    before = jnp.zeros((n, 1), f32)
-    for chunk in range(rows // LANES):
-        part = hot[:, chunk * LANES:(chunk + 1) * LANES]
-        count = jnp.dot(part.astype(bf16), upper, preferred_element_type=f32)
-        rank = jnp.sum(part * (count + before), axis=0, keepdims=True) - 1.0
-        before = before + count[:, LANES - 1:LANES]
-        place = lax.broadcasted_iota(jnp.int32, (LANES, LANES), 0)
-        slot_ref[:, chunk * LANES:(chunk + 1) * LANES] = (
-            (place == rank.astype(jnp.int32)).astype(f32).astype(bf16)
-        )
-    hot16 = hot.astype(bf16)
-    slots = slot_ref[...]
-    stack = []
-    for q in range(2):
-        stack += split(param_ref[q:q + 1, :], 3)
-    for q in range(2):
-        stack.append(span_ref[q:q + 1, :].astype(f32).astype(bf16))
-    out = nt_dot(jnp.concatenate([hot16 * part for part in stack], axis=0), slots)
-    out = [out[i * n:(i + 1) * n] for i in range(8)]
-    meta_send[pl.ds(0, n, stride=8), :] = out[0] + out[1] + out[2]
-    meta_send[pl.ds(1, n, stride=8), :] = out[3] + out[4] + out[5]
-    meta_send[pl.ds(2, n, stride=8), :] = out[6]
-    meta_send[pl.ds(3, n, stride=8), :] = out[7]
-    meta_send[pl.ds(4, n, stride=8), :] = jnp.zeros((n, LANES), f32)
-    meta_send[pl.ds(5, n, stride=8), :] = jnp.zeros((n, LANES), f32)
-    meta_send[pl.ds(6, n, stride=8), :] = jnp.zeros((n, LANES), f32)
-    meta_send[pl.ds(7, n, stride=8), :] = jnp.zeros((n, LANES), f32)
-
-    def block(number):
-        return pl.ds(pl.multiple_of(number * 8, 8), 8)
-
     def all_copy(src, dst, sems, other, landing):
         return pltpu.make_async_remote_copy(
-            src_ref=src.at[block(other)],
-            dst_ref=dst.at[block(landing)],
+            src_ref=src.at[other],
+            dst_ref=dst.at[landing],
             send_sem=sems[0].at[other],
             recv_sem=sems[1].at[landing],
             device_id=(other // ngy, lax.rem(other, ngy)),
@@ -224,7 +196,7 @@
             return carry
 
         lax.fori_loop(1, n, go, 0)
-        dst[block(me), :] = src[block(me), :]
+        dst[me] = src[me]
 
     def take_all(src, dst, sems):
         def go(i, carry):
@@ -243,7 +215,6 @@
 
     meta = (meta_send, meta_recv, (mssem, mrsem))
     surf = (surf_send, surf_recv, (ussem, ursem))
-    send_all(*meta)
 
     def fill(ix, carry):
         to = pl.multiple_of((ix + 2) * step + EDGE, 8)
@@ -251,25 +222,6 @@
         return carry
 
     lax.fori_loop(0, cx, fill, 0, unroll=UNROLL)
-    for side in range(4):
-        @pl.when(sides[side][0])
-        def _(side=side):
-            face_wait(0, side, send1.at[side], recv1).wait_recv()
-    for index in range(4):
-        @pl.when(corners[index][0])
-        def _(index=index):
-            corner_wait(index).wait_recv()
-    half = OMEGA / 2
-    for deep in range(2):
-        low, high = (1 - deep) * step + EDGE, (cx + 2 + deep) * step + EDGE
-        cpad[low:low + cy, :] = recv1[0, 3 + deep] * half
-        cpad[high:high + cy, :] = recv1[1, 3 + deep] * half
-        cpad[pl.ds(2 * step + EDGE - 1 - deep, cx, stride=step), :] = recv1[2, 3 + deep] * half
-        cpad[pl.ds(2 * step + EDGE + cy + deep, cx, stride=step), :] = recv1[3, 3 + deep] * half
-    for index in range(4):
-        row = (1 + (index // 2) * (cx + 1)) * step + EDGE - 1 + (index % 2) * (cy + 1)
-        cpad[row:row + 1, :] = crecv[index, 0:1] * half
-
     def inverse(center, others):
         lane = lax.broadcasted_iota(jnp.int32, center.shape, 1)
         above = jnp.where(lane == LANES - 1, 0.0, pltpu.roll(center, LANES - 1, 1))
@@ -300,24 +252,6 @@
         return carry
 
     lax.fori_loop(0, cx // UNROLL, scale, 0)
-
-    for side in range(4):
-        if side < 2:
-            at = (1 + side * (cx + 1)) * step + EDGE
-            inv, _ = inverse(
-                cpad[at:at + cy, :],
-                [cpad[at + d:at + d + cy, :] for d in (-step, step, -1, 1)],
-            )
-            for k in range(3):
-                y0[k, at - step + side * 0:at - step + cy, :] = recv1[side, k] * inv
-        else:
-            at = 2 * step + EDGE - 1 + (side - 2) * (cy + 1)
-            inv, _ = inverse(
-                cpad[pl.ds(at, cx, stride=step), :],
-                [cpad[pl.ds(at + d, cx, stride=step), :] for d in (-step, step, -1, 1)],
-            )
-            for k in range(3):
-                y0[k, pl.ds(at - step, cx, stride=step), :] = recv1[side, k] * inv
 
     def sweep(vsrc, vdst, ysrc, ydst):
         def layers(it, carry):
@@ -383,35 +317,122 @@
                 if ydst is not None:
                     ydst[k, pad, :] = ydst[k, pad, :] + more * inv
 
+    def line(kind, j, height):
+        if kind == 0:
+            base = (j + height) * step + EDGE
+            return lambda d: pl.ds(base + d, cy)
+        base = height * step + EDGE + j
+        return lambda d: pl.ds(base + d, cx, stride=step)
+
+    def flat_line(kind, j):
+        return pl.ds(j * cy, cy) if kind == 0 else pl.ds(j, cx, stride=cy)
+
+    def scale_line(kind, j):
+        c, flat, yl = line(kind, j, 2), flat_line(kind, j), line(kind, j, 1)
+        inv, _ = inverse(cpad[c(0), :], [cpad[c(d), :] for d in (-step, step, -1, 1)])
+        rd[flat, :] = inv
+        for k in range(3):
+            y0[k, yl(0), :] = vol[k, flat, :] * inv
+
+    def sweep_line(kind, j):
+        c, flat, yl = line(kind, j, 2), flat_line(kind, j), line(kind, j, 1)
+        center, up, inv = cpad[c(0), :], wz[flat, :], rd[flat, :]
+        weights = [(d, center + cpad[c(d), :]) for d in (step, -step, 1, -1)]
+        done = []
+        for k in range(3):
+            mid, first = y0[k, yl(0), :], vol[k, flat, :]
+            total = up * pltpu.roll(mid, LANES - 1, 1) + pltpu.roll(up * mid, 1, 1)
+            for d, weight in weights:
+                total = total + weight * y0[k, yl(d), :]
+            done.append(first + (1.0 - OMEGA) * first + total)
+        for k in range(3):
+            field[k, flat, :] = done[k]
+            y1[k, yl(0), :] = done[k] * inv
+
     sweep(vol, field, y0, y1)
+    for side in range(4):
+        @pl.when(sides[side][0])
+        def _(side=side):
+            face_wait(0, side, send1.at[side], recv1).wait_recv()
+    for index in range(4):
+        @pl.when(corners[index][0])
+        def _(index=index):
+            corner_wait(index).wait_recv()
+    half = OMEGA / 2
+    for deep in range(2):
+        low, high = (1 - deep) * step + EDGE, (cx + 2 + deep) * step + EDGE
+        cpad[low:low + cy, :] = recv1[0, 3 + deep] * half
+        cpad[high:high + cy, :] = recv1[1, 3 + deep] * half
+        cpad[pl.ds(2 * step + EDGE - 1 - deep, cx, stride=step), :] = recv1[2, 3 + deep] * half
+        cpad[pl.ds(2 * step + EDGE + cy + deep, cx, stride=step), :] = recv1[3, 3 + deep] * half
+    for index in range(4):
+        row = (1 + (index // 2) * (cx + 1)) * step + EDGE - 1 + (index % 2) * (cy + 1)
+        cpad[row:row + 1, :] = crecv[index, 0:1] * half
+
+    ends = ((0, 0), (0, cx - 1), (1, 0), (1, cy - 1))
+    beside = ((0, 1), (0, cx - 2), (1, 1), (1, cy - 2))
+    for kind, j in ends:
+        scale_line(kind, j)
+    for side in range(4):
+        if side < 2:
+            at = (1 + side * (cx + 1)) * step + EDGE
+            inv, _ = inverse(
+                cpad[at:at + cy, :],
+                [cpad[at + d:at + d + cy, :] for d in (-step, step, -1, 1)],
+            )
+            for k in range(3):
+                y0[k, at - step:at - step + cy, :] = recv1[side, k] * inv
+        else:
+            at = 2 * step + EDGE - 1 + (side - 2) * (cy + 1)
+            inv, _ = inverse(
+                cpad[pl.ds(at, cx, stride=step), :],
+                [cpad[pl.ds(at + d, cx, stride=step), :] for d in (-step, step, -1, 1)],
+            )
+            for k in range(3):
+                y0[k, pl.ds(at - step, cx, stride=step), :] = recv1[side, k] * inv
+
+    for kind, j in ends:
+        sweep_line(kind, j)
     send_faces(1, y1)
+    for kind, j in beside:
+        sweep_line(kind, j)
     sweep(field, val, y1, y2)
+    patch = patch_ref[...]
+    hot = (lax.broadcasted_iota(jnp.int32, (n, rows), 0) == patch).astype(f32)
+    hot_ref[...] = hot
+    upper = (
+        lax.broadcasted_iota(jnp.int32, (LANES, LANES), 0)
+        <= lax.broadcasted_iota(jnp.int32, (LANES, LANES), 1)
+    ).astype(f32).astype(bf16)
+    before = jnp.zeros((n, 1), f32)
+    for chunk in range(rows // LANES):
+        part = hot[:, chunk * LANES:(chunk + 1) * LANES]
+        count = jnp.dot(part.astype(bf16), upper, preferred_element_type=f32)
+        rank = jnp.sum(part * (count + before), axis=0, keepdims=True) - 1.0
+        before = before + count[:, LANES - 1:LANES]
+        place = lax.broadcasted_iota(jnp.int32, (LANES, LANES), 0)
+        slot_ref[:, chunk * LANES:(chunk + 1) * LANES] = (
+            (place == rank.astype(jnp.int32)).astype(f32).astype(bf16)
+        )
     add_faces(1, val, y2)
     send_faces(2, y2)
     sweep(val, field, y2, None)
-
-    take_all(*meta)
-    basis_u = pieces(meta_recv[pl.ds(0, n, stride=8), :])
-    basis_v = pieces(meta_recv[pl.ds(1, n, stride=8), :])
-    span_u = meta_recv[pl.ds(2, n, stride=8), :].astype(jnp.int32)
-    span_v = meta_recv[pl.ds(3, n, stride=8), :].astype(jnp.int32)
-    knot = lax.broadcasted_iota(jnp.int32, (NC, LANES), 0)
-
-    def spline(span, basis, d):
-        offset = knot - span[d:d + 1, :]
-        out = jnp.where(offset == 0, basis[0][d:d + 1, :], 0.0)
-        for index in range(1, 4):
-            out = jnp.where(offset == index, basis[index][d:d + 1, :], out)
-        return out
-
-    for d in range(n):
-        lanes = slice(d * LANES, (d + 1) * LANES)
-        bu_ref[:, lanes] = spline(span_u, basis_u, d)
-        high, low = split(spline(span_v, basis_v, d), 2)
-        bv_ref[:NC, lanes] = high
-        bv_ref[NC:, lanes] = low
-
+    hot16 = hot_ref[...].astype(bf16)
+    slots = slot_ref[...]
+    stack = []
+    for q in range(2):
+        stack += split(param_ref[q:q + 1, :], 3)
+    for q in range(2):
+        stack.append(span_ref[q:q + 1, :].astype(f32).astype(bf16))
+    out = nt_dot(jnp.concatenate([hot16 * part for part in stack], axis=0), slots)
+    out = [out[i * n:(i + 1) * n] for i in range(8)]
+    meta_send[:, 0, :] = out[0] + out[1] + out[2]
+    meta_send[:, 1, :] = out[3] + out[4] + out[5]
+    meta_send[:, 2, :] = out[6]
+    meta_send[:, 3, :] = out[7]
+    send_all(*meta)
     add_faces(2, field, None)
+
 
     def surface(ix, carry):
         to = pl.ds(pl.multiple_of(ix * cy, 8), cy)
@@ -435,31 +456,32 @@
     out = nt_dot(jnp.concatenate([hot16 * part for part in stack], axis=0), slots)
     out = [out[i * n:(i + 1) * n] for i in range(9)]
     for k in range(3):
-        surf_send[pl.ds(k, n, stride=8), :] = out[3 * k] + out[3 * k + 1] + out[3 * k + 2]
-    for k in range(3, 8):
-        surf_send[pl.ds(k, n, stride=8), :] = jnp.zeros((n, LANES), f32)
+        surf_send[:, k, :] = out[3 * k] + out[3 * k + 1] + out[3 * k + 2]
+    surf_send[:, 3, :] = jnp.zeros((n, LANES), f32)
     send_all(*surf)
+
+    take_all(*meta)
+    basis_u = pieces(meta_recv[:, 0, :])
+    basis_v = pieces(meta_recv[:, 1, :])
+    span_u = meta_recv[:, 2, :].astype(jnp.int32)
+    span_v = meta_recv[:, 3, :].astype(jnp.int32)
+    knot = lax.broadcasted_iota(jnp.int32, (NC, LANES), 0)
+
+    def spline(span, basis, d):
+        offset = knot - span[d:d + 1, :]
+        out = jnp.where(offset == 0, basis[0][d:d + 1, :], 0.0)
+        for index in range(1, 4):
+            out = jnp.where(offset == index, basis[index][d:d + 1, :], out)
+        return out
+
+    for d in range(n):
+        lanes = slice(d * LANES, (d + 1) * LANES)
+        bu_ref[:, lanes] = spline(span_u, basis_u, d)
+        high, low = split(spline(span_v, basis_v, d), 2)
+        bv_ref[:NC, lanes] = high
+        bv_ref[NC:, lanes] = low
+
     take_all(*surf)
-
-    group = 8
-    total = jnp.zeros((6 * NC, 2 * NC), f32)
-    for first in range(0, n, group):
-        lanes = slice(first * LANES, (first + group) * LANES)
-        bu = bu_ref[:, lanes]
-        left = jnp.concatenate(
-            [
-                bu * jnp.concatenate(
-                    [surf_recv[d * 8 + k:d * 8 + k + 1, :] for d in range(first, first + group)],
-                    axis=1,
-                )
-                for k in range(3)
-            ],
-            axis=0,
-        )
-        total = total + nt_dot(jnp.concatenate(split(left, 2), axis=0), bv_ref[:, lanes])
-    for k in range(3):
-        high, low = total[k * NC:(k + 1) * NC], total[(3 + k) * NC:(4 + k) * NC]
-        grad_ref[k] = high[:, :NC] + high[:, NC:] + low[:, :NC] + low[:, NC:]
 
     for side in range(4):
         @pl.when(sides[side][0])
@@ -475,6 +497,31 @@
     sent_all(*surf)
 
 
+def product(n, val, surf_ref, bu_ref, bv_ref, field, grad_ref, sem):
+    store = pltpu.make_async_copy(val, field, sem)
+    store.start()
+    group = 8
+    total = jnp.zeros((6 * NC, 2 * NC), jnp.float32)
+    for first in range(0, n, group):
+        lanes = slice(first * LANES, (first + group) * LANES)
+        bu = bu_ref[:, lanes]
+        left = jnp.concatenate(
+            [
+                bu * jnp.concatenate(
+                    [surf_ref[d, k:k + 1, :] for d in range(first, first + group)],
+                    axis=1,
+                )
+                for k in range(3)
+            ],
+            axis=0,
+        )
+        total = total + nt_dot(jnp.concatenate(split(left, 2), axis=0), bv_ref[:, lanes])
+    for k in range(3):
+        high, low = total[k * NC:(k + 1) * NC], total[(3 + k) * NC:(4 + k) * NC]
+        grad_ref[k] = high[:, :NC] + high[:, NC:] + low[:, :NC] + low[:, NC:]
+    store.wait()
+
+
 def body(volume_sens, stiffness, patch_of_row, knot_spans, span_params):
     ngx, ngy = lax.axis_size("gx"), lax.axis_size("gy")
     n = ngx * ngy
@@ -483,11 +530,15 @@
     step = cy + 2 * EDGE
     f32, bf16 = jnp.float32, jnp.bfloat16
     dma = pltpu.SemaphoreType.DMA
-    field, grads = pl.pallas_call(
+    vmem = pl.BlockSpec(memory_space=pltpu.VMEM)
+    room = 62 * 2**20 - 4 * (3 * rows * nz + n * 4 * LANES + 2 * NC * n * LANES)
+    found = pl.pallas_call(
         functools.partial(kernel, (ngx, ngy, cx, cy, rows)),
         out_shape=(
             pltpu.VMEM((3, rows, nz), f32),
-            pltpu.VMEM((3, NC, NC), f32),
+            pltpu.VMEM((n, 4, LANES), f32),
+            pltpu.VMEM((NC, n * LANES), f32),
+            pltpu.VMEM((2 * NC, n * LANES), bf16),
         ),
         in_specs=[
             pl.BlockSpec(memory_space=pl.ANY),
@@ -496,10 +547,7 @@
             pl.BlockSpec(memory_space=pltpu.VMEM),
             pl.BlockSpec(memory_space=pltpu.VMEM),
         ],
-        out_specs=(
-            pl.BlockSpec(memory_space=pltpu.VMEM),
-            pl.BlockSpec(memory_space=pltpu.VMEM),
-        ),
+        out_specs=(vmem,) * 4,
         scratch_shapes=[
             pltpu.VMEM((3, rows, nz), f32),
             pltpu.VMEM((rows, nz), f32),
@@ -519,12 +567,9 @@
             pltpu.VMEM((n, rows), f32),
             pltpu.VMEM((LANES, rows), bf16),
             pltpu.VMEM((rows, nz), f32),
-            pltpu.VMEM((n * 8, LANES), f32),
-            pltpu.VMEM((n * 8, LANES), f32),
-            pltpu.VMEM((n * 8, LANES), f32),
-            pltpu.VMEM((n * 8, LANES), f32),
-            pltpu.VMEM((NC, n * LANES), f32),
-            pltpu.VMEM((2 * NC, n * LANES), bf16),
+            pltpu.VMEM((n, 4, LANES), f32),
+            pltpu.VMEM((n, 4, LANES), f32),
+            pltpu.VMEM((n, 4, LANES), f32),
             dma((2,)),
             dma((12,)),
             dma((12,)),
@@ -536,7 +581,7 @@
             dma((n,)),
         ],
         compiler_params=pltpu.CompilerParams(
-            collective_id=0, has_side_effects=True, vmem_limit_bytes=56 * 2**20
+            collective_id=0, has_side_effects=True, vmem_limit_bytes=room
         ),
     )(
         volume_sens.reshape(3, rows, nz),
@@ -545,6 +590,17 @@
         knot_spans[0].T,
         span_params[0].T,
     )
+    field, grads = pl.pallas_call(
+        functools.partial(product, n),
+        out_shape=(
+            jax.ShapeDtypeStruct((3, rows, nz), f32),
+            jax.ShapeDtypeStruct((3, NC, NC), f32),
+        ),
+        in_specs=[vmem] * 4,
+        out_specs=(pl.BlockSpec(memory_space=pl.ANY), vmem),
+        scratch_shapes=[dma],
+        compiler_params=pltpu.CompilerParams(vmem_limit_bytes=32 * 2**20),
+    )(*found)
     return field.reshape(volume_sens.shape), grads[None]
 
 

time: 37.1 us -> 32.7 us (0.88)
  Pallas kernels: 34.4 us -> 31.8 us
  local copies, waits for them, and re-layouts: 1.79 us -> 0 us
    pallas_call x1, Pallas kernels: 34.4 us -> 29.9 us  [body(): pl.pallas_call(functools.partial(kernel, (ngx, ngy, cx, cy, rows)), out_s...]
    pallas_call x0 -> x1, Pallas kernels: none -> 1.85 us  [body(): pl.pallas_call(functools.partial(product, n), out_shape=(jax.ShapeDtypeSt...]
    unnamed x2 -> x0, local copies, waits for them, and re-layouts: 1.79 us -> none
where the time goes in v3:
time: 32.7 us; the launch traced here: 32.4 us
  Pallas kernels  31.8 us (97%)
  between operations  0.64 us (2%)
    pallas_call x1, Pallas kernels, body(): pl.pallas_call(functools.partial(kernel, (ngx, ngy, cx, cy, rows)), out_s...  29.9 us
    pallas_call x1, Pallas kernels, body(): pl.pallas_call(functools.partial(product, n), out_shape=(jax.ShapeDtypeSt...  1.85 us

profile of v3, /device:TPU:0, one launch (start us, length us, event | category | flops | bytes accessed | tf_op | source)
XLA Modules:
  0.0 32.4 jit_solution(14329278235206823074)
XLA Ops:
  0.6 29.9 %shard_map.68 = (f32[3,1024,128]{2,1,0:T(8,128)S(1)}, f32[32,4,128]{2,1,0:T(4,128)S(1)}, f32[64,4096]{1,0:T(8,128)S(1)}, bf16[128,4096]{1,0:T(8,128)(2,1)S(1)}) custom-call(f32[3,1024,128]{2,1,0:T(8,128)} %bitcast.11, f32[1024,128]{1,0:T(8,128)} %bitcast.12, s32[1,1024]{1,0:T(1,128)} %bitcast.15, s32[2,1024]{1,0:T(2,128)} %bitcast.13, f32[2,1024]{1,0:T(2,128)} %bitcast.14), custom_call_target="tpu_custom_call" | custom-call | tf_op jit(solution)/shard_map/pallas_call | solution.py:535
  30.6 1.8 %shard_map.69 = (f32[3,1024,128]{2,1,0:T(8,128)}, f32[3,64,64]{2,1,0:T(8,128)}) custom-call(f32[3,1024,128]{2,1,0:T(8,128)S(1)} %get-tuple-element.8.val, f32[32,4,128]{2,1,0:T(4,128)S(1)} %get-tuple-element.9.surf_ref, f32[64,4096]{1,0:T(8,128)S(1)} %get-tuple-element.10.bu_ref, bf16[128,4096]{1,0:T(8,128)(2,1)S(1)} %get-tuple-element.11.bv_ref), custom_call_target="tpu_custom_call" | custom-call | tf_op jit(solution)/shard_map/pallas_call | solution.py:593

commit v4 on v3

--- a/solution.py
+++ b/solution.py
@@ -48,7 +48,7 @@
     field, surf_recv, bu_ref, bv_ref,
     vol, cin, cpad, rd, wz, val, y0, y1, y2,
     send1, recv1, csend, crecv, send_y, recv23,
-    hot_ref, slot_ref, xcol,
+    hot_ref, slot_ref, xcol, face_w, face_i, hot_face, slot_face,
     meta_send, meta_recv, surf_send,
     in_sem, ssem, rsem, cssem, crsem, mssem, mrsem, ussem, ursem,
 ):
@@ -60,9 +60,10 @@
     f32, bf16 = jnp.float32, jnp.bfloat16
 
     load_c = pltpu.make_async_copy(stiff_hbm, cin, in_sem.at[0])
-    load_v = pltpu.make_async_copy(vol_hbm, vol, in_sem.at[1])
+    load_v = [pltpu.make_async_copy(vol_hbm.at[k], vol.at[k], in_sem.at[1 + k]) for k in range(3)]
     load_c.start()
-    load_v.start()
+    for k in range(3):
+        load_v[k].start()
 
     barrier = pltpu.get_barrier_semaphore()
 
@@ -154,13 +155,7 @@
         cpad[pl.ds(layer * step + EDGE, cy), :] = jnp.zeros((cy, LANES), f32)
 
     load_c.wait()
-    load_v.wait()
     last = (cx - 1) * cy
-    for k in range(3):
-        send1[0, k] = vol[k, 0:cy]
-        send1[1, k] = vol[k, last:last + cy]
-        send1[2, k] = vol[k, pl.ds(0, cx, stride=cy)]
-        send1[3, k] = vol[k, pl.ds(cy - 1, cx, stride=cy)]
     for deep in range(2):
         send1[0, 3 + deep] = cin[deep * cy:(deep + 1) * cy]
         send1[1, 3 + deep] = cin[last - deep * cy:last - deep * cy + cy]
@@ -170,8 +165,15 @@
         row = (index // 2) * last + (index % 2) * (cy - 1)
         csend[index] = jnp.broadcast_to(cin[row:row + 1], (8, LANES))
 
+    for k in range(3):
+        load_v[k].wait()
+        send1[0, k] = vol[k, 0:cy]
+        send1[1, k] = vol[k, last:last + cy]
+        send1[2, k] = vol[k, pl.ds(0, cx, stride=cy)]
+        send1[3, k] = vol[k, pl.ds(cy - 1, cx, stride=cy)]
+
     pl.semaphore_wait(barrier, n - 1)
-    for side in range(4):
+    for side in (2, 3, 0, 1):
         @pl.when(sides[side][0])
         def _(side=side):
             face_copy(0, side, send1.at[side], recv1).start()
@@ -184,8 +186,8 @@
         return pltpu.make_async_remote_copy(
             src_ref=src.at[other],
             dst_ref=dst.at[landing],
-            send_sem=sems[0].at[other],
-            recv_sem=sems[1].at[landing],
+            send_sem=sems[0],
+            recv_sem=sems[1],
             device_id=(other // ngy, lax.rem(other, ngy)),
             device_id_type=MESH,
         )
@@ -198,20 +200,16 @@
         lax.fori_loop(1, n, go, 0)
         dst[me] = src[me]
 
-    def take_all(src, dst, sems):
-        def go(i, carry):
-            other = lax.rem(me + i, n)
-            all_copy(src, dst, sems, other, other).wait_recv()
-            return carry
-
-        lax.fori_loop(1, n, go, 0)
-
-    def sent_all(src, dst, sems):
-        def go(i, carry):
-            all_copy(src, dst, sems, lax.rem(me + i, n), me).wait_send()
-            return carry
-
-        lax.fori_loop(1, n, go, 0)
+    def every(src, dst, sems):
+        other = lax.rem(me + 1, n)
+        return pltpu.make_async_remote_copy(
+            src_ref=src.at[pl.ds(0, n - 1)],
+            dst_ref=dst.at[pl.ds(0, n - 1)],
+            send_sem=sems[0],
+            recv_sem=sems[1],
+            device_id=(other // ngy, lax.rem(other, ngy)),
+            device_id_type=MESH,
+        )
 
     meta = (meta_send, meta_recv, (mssem, mrsem))
     surf = (surf_send, surf_recv, (ussem, ursem))
@@ -278,45 +276,6 @@
 
         lax.fori_loop(0, cx // UNROLL, layers, 0)
 
-    def send_faces(turn, y):
-        low, high = step + EDGE, cx * step + EDGE
-        for k in range(3):
-            send_y[turn - 1, 2, k] = y[k, pl.ds(low, cx, stride=step), :]
-            send_y[turn - 1, 3, k] = y[k, pl.ds(low + cy - 1, cx, stride=step), :]
-            send_y[turn - 1, 0, k] = y[k, low:low + cy, :]
-            send_y[turn - 1, 1, k] = y[k, high:high + cy, :]
-        for side in range(4):
-            @pl.when(sides[side][0])
-            def _(side=side):
-                face_copy(turn, side, send_y.at[turn - 1, side], recv23.at[turn - 1]).start()
-
-    def add_faces(turn, val, ydst):
-        for side in range(4):
-            @pl.when(sides[side][0])
-            def _(side=side):
-                face_wait(turn, side, send_y.at[turn - 1, side], recv23.at[turn - 1]).wait_recv()
-        for side in range(4):
-            if side < 2:
-                ct = (2 + side * (cx - 1)) * step + EDGE
-                to = side * last
-                outer = ct + (step if side else -step)
-                here, there, flat = pl.ds(ct, cy), pl.ds(outer, cy), pl.ds(to, cy)
-                pad = pl.ds(ct - step, cy)
-            else:
-                shift = (side - 2) * (cy - 1)
-                ct = 2 * step + EDGE + shift
-                outer = ct + (1 if side == 3 else -1)
-                here, there = pl.ds(ct, cx, stride=step), pl.ds(outer, cx, stride=step)
-                flat = pl.ds(shift, cx, stride=cy)
-                pad = pl.ds(ct - step, cx, stride=step)
-            weight = cpad[here, :] + cpad[there, :]
-            inv = rd[flat, :]
-            for k in range(3):
-                more = weight * recv23[turn - 1, side, k]
-                val[k, flat, :] = val[k, flat, :] + more
-                if ydst is not None:
-                    ydst[k, pad, :] = ydst[k, pad, :] + more * inv
-
     def line(kind, j, height):
         if kind == 0:
             base = (j + height) * step + EDGE
@@ -334,7 +293,7 @@
         for k in range(3):
             y0[k, yl(0), :] = vol[k, flat, :] * inv
 
-    def sweep_line(kind, j):
+    def sweep_line(kind, j, side=None):
         c, flat, yl = line(kind, j, 2), flat_line(kind, j), line(kind, j, 1)
         center, up, inv = cpad[c(0), :], wz[flat, :], rd[flat, :]
         weights = [(d, center + cpad[c(d), :]) for d in (step, -step, 1, -1)]
@@ -348,6 +307,29 @@
         for k in range(3):
             field[k, flat, :] = done[k]
             y1[k, yl(0), :] = done[k] * inv
+            if side is not None:
+                send_y[0, side, k] = done[k] * inv
+        if side is not None:
+            send_face(1, side)
+
+    def send_face(turn, side):
+        @pl.when(sides[side][0])
+        def _():
+            face_copy(turn, side, send_y.at[turn - 1, side], recv23.at[turn - 1]).start()
+
+    def take_face(turn, side):
+        @pl.when(sides[side][0])
+        def _():
+            face_wait(turn, side, send_y.at[turn - 1, side], recv23.at[turn - 1]).wait_recv()
+
+    ends = ((0, 0), (0, cx - 1), (1, 0), (1, cy - 1))
+    beside = ((0, 1), (0, cx - 2), (1, 1), (1, cy - 2))
+
+    def add_values(turn, dst):
+        for side in range(4):
+            flat = flat_line(*ends[side])
+            for k in range(3):
+                dst[k, flat, :] = dst[k, flat, :] + face_w[side] * recv23[turn - 1, side, k]
 
     sweep(vol, field, y0, y1)
     for side in range(4):
@@ -369,8 +351,6 @@
         row = (1 + (index // 2) * (cx + 1)) * step + EDGE - 1 + (index % 2) * (cy + 1)
         cpad[row:row + 1, :] = crecv[index, 0:1] * half
 
-    ends = ((0, 0), (0, cx - 1), (1, 0), (1, cy - 1))
-    beside = ((0, 1), (0, cx - 2), (1, 1), (1, cy - 2))
     for kind, j in ends:
         scale_line(kind, j)
     for side in range(4):
@@ -391,11 +371,15 @@
             for k in range(3):
                 y0[k, pl.ds(at - step, cx, stride=step), :] = recv1[side, k] * inv
 
-    for kind, j in ends:
-        sweep_line(kind, j)
-    send_faces(1, y1)
+    for side in (2, 3, 0, 1):
+        sweep_line(*ends[side], side)
     for kind, j in beside:
         sweep_line(kind, j)
+    for side, out in enumerate((-step, step, -1, 1)):
+        at = line(*ends[side], 2)
+        weight = cpad[at(0), :] + cpad[at(out), :]
+        face_w[side] = weight
+        face_i[side] = weight * rd[flat_line(*ends[side]), :]
     sweep(field, val, y1, y2)
     patch = patch_ref[...]
     hot = (lax.broadcasted_iota(jnp.int32, (n, rows), 0) == patch).astype(f32)
@@ -414,24 +398,46 @@
         slot_ref[:, chunk * LANES:(chunk + 1) * LANES] = (
             (place == rank.astype(jnp.int32)).astype(f32).astype(bf16)
         )
-    add_faces(1, val, y2)
-    send_faces(2, y2)
+    face = lax.broadcasted_iota(jnp.int32, (rows, LANES), 1)
+    part = face % cy
+    where = jnp.where(face < cy, part, last + part)
+    where = jnp.where(face >= 2 * cy, part * cy, where)
+    where = jnp.where(face >= 3 * cy, part * cy + cy - 1, where)
+    pick = (lax.broadcasted_iota(jnp.int32, (rows, LANES), 0) == where).astype(f32).astype(bf16)
+    hot_face[...] = jnp.dot(hot.astype(bf16), pick, preferred_element_type=f32)
+    slot_face[...] = jnp.dot(slot_ref[...], pick, preferred_element_type=f32).astype(bf16)
+
+    for side in (0, 1, 2, 3):
+        take_face(1, side)
+        at = line(*ends[side], 1)(0)
+        for k in range(3):
+            new = y2[k, at, :] + face_i[side] * recv23[0, side, k]
+            y2[k, at, :] = new
+            if side > 1:
+                send_y[1, side, k] = new
+        if side > 1:
+            send_face(2, side)
+    for side in (0, 1):
+        at = line(*ends[side], 1)(0)
+        for k in range(3):
+            send_y[1, side, k] = y2[k, at, :]
+        send_face(2, side)
+    add_values(1, val)
     sweep(val, field, y2, None)
     hot16 = hot_ref[...].astype(bf16)
     slots = slot_ref[...]
     stack = []
     for q in range(2):
-        stack += split(param_ref[q:q + 1, :], 3)
+        stack += split(param_ref[q:q + 1, :], 2)
     for q in range(2):
         stack.append(span_ref[q:q + 1, :].astype(f32).astype(bf16))
     out = nt_dot(jnp.concatenate([hot16 * part for part in stack], axis=0), slots)
-    out = [out[i * n:(i + 1) * n] for i in range(8)]
-    meta_send[:, 0, :] = out[0] + out[1] + out[2]
-    meta_send[:, 1, :] = out[3] + out[4] + out[5]
-    meta_send[:, 2, :] = out[6]
-    meta_send[:, 3, :] = out[7]
+    out = [out[i * n:(i + 1) * n] for i in range(6)]
+    meta_send[:, 0, :] = out[0] + out[1]
+    meta_send[:, 1, :] = out[2] + out[3]
+    meta_send[:, 2, :] = out[4]
+    meta_send[:, 3, :] = out[5]
     send_all(*meta)
-    add_faces(2, field, None)
 
 
     def surface(ix, carry):
@@ -448,19 +454,33 @@
     surf_rows = jnp.concatenate(
         [xcol[c * LANES:(c + 1) * LANES, :].T[0:8] for c in range(rows // LANES)], axis=1
     )
-    hot16 = hot_ref[...].astype(bf16)
-    slots = slot_ref[...]
-    stack = []
+    def route(values, hot16, slots):
+        stack = []
+        for k in range(3):
+            stack += split(values[k:k + 1, :], 2)
+        out = nt_dot(jnp.concatenate([hot16 * part for part in stack], axis=0), slots)
+        return [out[2 * k * n:(2 * k + 1) * n] + out[(2 * k + 1) * n:(2 * k + 2) * n] for k in range(3)]
+
+    most = route(surf_rows, hot_ref[...].astype(bf16), slot_ref[...])
     for k in range(3):
-        stack += split(surf_rows[k:k + 1, :], 3)
-    out = nt_dot(jnp.concatenate([hot16 * part for part in stack], axis=0), slots)
-    out = [out[i * n:(i + 1) * n] for i in range(9)]
+        surf_send[:, k, :] = most[k]
+    surf_send[:, 3, :] = jnp.zeros((n, LANES), f32)
+
+    lane = lax.broadcasted_iota(jnp.int32, (cy, LANES), 1)
+    for side in range(4):
+        take_face(2, side)
+        weight = face_i[side] * OMEGA
+        out = jnp.where(lane == 0, weight * recv23[1, side, 0], 0.0)
+        for k in (1, 2):
+            out = jnp.where(lane == k, pltpu.roll(weight * recv23[1, side, k], k, 1), out)
+        xcol[side * cy:(side + 1) * cy, :] = out
+    more = route(xcol[0:LANES, :].T[0:8], hot_face[...].astype(bf16), slot_face[...])
     for k in range(3):
-        surf_send[:, k, :] = out[3 * k] + out[3 * k + 1] + out[3 * k + 2]
-    surf_send[:, 3, :] = jnp.zeros((n, LANES), f32)
+        surf_send[:, k, :] = surf_send[:, k, :] + more[k]
     send_all(*surf)
-
-    take_all(*meta)
+    add_values(2, field)
+
+    every(*meta).wait_recv()
     basis_u = pieces(meta_recv[:, 0, :])
     basis_v = pieces(meta_recv[:, 1, :])
     span_u = meta_recv[:, 2, :].astype(jnp.int32)
@@ -481,7 +501,6 @@
         bv_ref[:NC, lanes] = high
         bv_ref[NC:, lanes] = low
 
-    take_all(*surf)
 
     for side in range(4):
         @pl.when(sides[side][0])
@@ -493,8 +512,9 @@
         @pl.when(corners[index][0])
         def _(index=index):
             corner_copy(index).wait_send()
-    sent_all(*meta)
-    sent_all(*surf)
+    every(*meta).wait_send()
+    every(*surf).wait_recv()
+    every(*surf).wait_send()
 
 
 def product(n, val, surf_ref, bu_ref, bv_ref, field, grad_ref, sem):
@@ -567,18 +587,22 @@
             pltpu.VMEM((n, rows), f32),
             pltpu.VMEM((LANES, rows), bf16),
             pltpu.VMEM((rows, nz), f32),
+            pltpu.VMEM((4, cy, nz), f32),
+            pltpu.VMEM((4, cy, nz), f32),
+            pltpu.VMEM((n, LANES), f32),
+            pltpu.VMEM((LANES, LANES), bf16),
             pltpu.VMEM((n, 4, LANES), f32),
             pltpu.VMEM((n, 4, LANES), f32),
             pltpu.VMEM((n, 4, LANES), f32),
-            dma((2,)),
+            dma((4,)),
             dma((12,)),
             dma((12,)),
             dma((4,)),
             dma((4,)),
-            dma((n,)),
-            dma((n,)),
-            dma((n,)),
-            dma((n,)),
+            dma,
+            dma,
+            dma,
+            dma,
         ],
         compiler_params=pltpu.CompilerParams(
             collective_id=0, has_side_effects=True, vmem_limit_bytes=room

time: 32.7 us -> 29.3 us (0.90)
  Pallas kernels: 31.8 us -> 28.4 us
    pallas_call x1, Pallas kernels: 29.9 us -> 26.5 us  [body(): pl.pallas_call(functools.partial(kernel, (ngx, ngy, cx, cy, rows)), out_s...]
where the time goes in v4:
time: 29.3 us; the launch traced here: 29 us
  Pallas kernels  28.4 us (97%)
  between operations  0.64 us (2%)
    pallas_call x1, Pallas kernels, body(): pl.pallas_call(functools.partial(kernel, (ngx, ngy, cx, cy, rows)), out_s...  26.5 us
    pallas_call x1, Pallas kernels, body(): pl.pallas_call(functools.partial(product, n), out_shape=(jax.ShapeDtypeSt...  1.85 us

profile of v4, /device:TPU:0, one launch (start us, length us, event | category | flops | bytes accessed | tf_op | source)
XLA Modules:
  0.0 29.0 jit_solution(13939426883057250890)
XLA Ops:
  0.6 26.5 %shard_map.68 = (f32[3,1024,128]{2,1,0:T(8,128)S(1)}, f32[32,4,128]{2,1,0:T(4,128)S(1)}, f32[64,4096]{1,0:T(8,128)S(1)}, bf16[128,4096]{1,0:T(8,128)(2,1)S(1)}) custom-call(f32[3,1024,128]{2,1,0:T(8,128)} %bitcast.11, f32[1024,128]{1,0:T(8,128)} %bitcast.12, s32[1,1024]{1,0:T(1,128)} %bitcast.15, s32[2,1024]{1,0:T(2,128)} %bitcast.13, f32[2,1024]{1,0:T(2,128)} %bitcast.14), custom_call_target="tpu_custom_call" | custom-call | tf_op jit(solution)/shard_map/pallas_call | solution.py:555
  27.2 1.8 %shard_map.69 = (f32[3,1024,128]{2,1,0:T(8,128)}, f32[3,64,64]{2,1,0:T(8,128)}) custom-call(f32[3,1024,128]{2,1,0:T(8,128)S(1)} %get-tuple-element.8.val, f32[32,4,128]{2,1,0:T(4,128)S(1)} %get-tuple-element.9.surf_ref, f32[64,4096]{1,0:T(8,128)S(1)} %get-tuple-element.10.bu_ref, bf16[128,4096]{1,0:T(8,128)(2,1)S(1)} %get-tuple-element.11.bv_ref), custom_call_target="tpu_custom_call" | custom-call | tf_op jit(solution)/shard_map/pallas_call | solution.py:617

commit v5 on v4

--- a/solution.py
+++ b/solution.py
@@ -12,7 +12,7 @@
 OMEGA = 2.0 / 3.0
 LANES = 128
 EDGE = 8
-UNROLL = 4
+UNROLL = 8
 MESH = pl.DeviceIdType.MESH
 NT = (((1,), (1,)), ((), ()))
 
@@ -44,12 +44,12 @@
 
 def kernel(
     sizes,
-    vol_hbm, stiff_hbm, patch_ref, span_ref, param_ref,
+    vol_hbm, stiff_hbm, patch_hbm, span_hbm, param_hbm,
     field, surf_recv, bu_ref, bv_ref,
     vol, cin, cpad, rd, wz, val, y0, y1, y2,
     send1, recv1, csend, crecv, send_y, recv23,
     hot_ref, slot_ref, xcol, face_w, face_i, hot_face, slot_face,
-    meta_send, meta_recv, surf_send,
+    patch_ref, span_ref, param_ref, meta_send, meta_recv, surf_send,
     in_sem, ssem, rsem, cssem, crsem, mssem, mrsem, ussem, ursem,
 ):
     ngx, ngy, cx, cy, rows = sizes
@@ -61,9 +61,18 @@
 
     load_c = pltpu.make_async_copy(stiff_hbm, cin, in_sem.at[0])
     load_v = [pltpu.make_async_copy(vol_hbm.at[k], vol.at[k], in_sem.at[1 + k]) for k in range(3)]
+    load_rows = [
+        pltpu.make_async_copy(src, dst, in_sem.at[4 + i])
+        for i, (src, dst) in enumerate(
+            ((patch_hbm, patch_ref), (span_hbm, span_ref), (param_hbm, param_ref))
+        )
+    ]
+    load_rows[0].start()
     load_c.start()
     for k in range(3):
         load_v[k].start()
+    load_rows[1].start()
+    load_rows[2].start()
 
     barrier = pltpu.get_barrier_semaphore()
 
@@ -153,6 +162,25 @@
         y[:, pl.ds((cx + 1) * step + EDGE, cy), :] = jnp.zeros((3, cy, LANES), f32)
     for layer in (0, 1, cx + 2, cx + 3):
         cpad[pl.ds(layer * step + EDGE, cy), :] = jnp.zeros((cy, LANES), f32)
+
+    load_rows[0].wait()
+    patch = patch_ref[...]
+    hot = (lax.broadcasted_iota(jnp.int32, (n, rows), 0) == patch).astype(f32)
+    hot_ref[...] = hot
+    upper = (
+        lax.broadcasted_iota(jnp.int32, (LANES, LANES), 0)
+        <= lax.broadcasted_iota(jnp.int32, (LANES, LANES), 1)
+    ).astype(f32).astype(bf16)
+    before = jnp.zeros((n, 1), f32)
+    for chunk in range(rows // LANES):
+        part = hot[:, chunk * LANES:(chunk + 1) * LANES]
+        count = jnp.dot(part.astype(bf16), upper, preferred_element_type=f32)
+        rank = jnp.sum(part * (count + before), axis=0, keepdims=True) - 1.0
+        before = before + count[:, LANES - 1:LANES]
+        place = lax.broadcasted_iota(jnp.int32, (LANES, LANES), 0)
+        slot_ref[:, chunk * LANES:(chunk + 1) * LANES] = (
+            (place == rank.astype(jnp.int32)).astype(f32).astype(bf16)
+        )
 
     load_c.wait()
     last = (cx - 1) * cy
@@ -381,31 +409,31 @@
         face_w[side] = weight
         face_i[side] = weight * rd[flat_line(*ends[side]), :]
     sweep(field, val, y1, y2)
-    patch = patch_ref[...]
-    hot = (lax.broadcasted_iota(jnp.int32, (n, rows), 0) == patch).astype(f32)
-    hot_ref[...] = hot
-    upper = (
-        lax.broadcasted_iota(jnp.int32, (LANES, LANES), 0)
-        <= lax.broadcasted_iota(jnp.int32, (LANES, LANES), 1)
-    ).astype(f32).astype(bf16)
-    before = jnp.zeros((n, 1), f32)
-    for chunk in range(rows // LANES):
-        part = hot[:, chunk * LANES:(chunk + 1) * LANES]
-        count = jnp.dot(part.astype(bf16), upper, preferred_element_type=f32)
-        rank = jnp.sum(part * (count + before), axis=0, keepdims=True) - 1.0
-        before = before + count[:, LANES - 1:LANES]
-        place = lax.broadcasted_iota(jnp.int32, (LANES, LANES), 0)
-        slot_ref[:, chunk * LANES:(chunk + 1) * LANES] = (
-            (place == rank.astype(jnp.int32)).astype(f32).astype(bf16)
-        )
-    face = lax.broadcasted_iota(jnp.int32, (rows, LANES), 1)
-    part = face % cy
+    face = lax.broadcasted_iota(jnp.int32, (1, LANES), 1)
+    part = lax.rem(face, cy)
     where = jnp.where(face < cy, part, last + part)
     where = jnp.where(face >= 2 * cy, part * cy, where)
     where = jnp.where(face >= 3 * cy, part * cy + cy - 1, where)
     pick = (lax.broadcasted_iota(jnp.int32, (rows, LANES), 0) == where).astype(f32).astype(bf16)
-    hot_face[...] = jnp.dot(hot.astype(bf16), pick, preferred_element_type=f32)
+    hot_face[...] = jnp.dot(hot_ref[...].astype(bf16), pick, preferred_element_type=f32)
     slot_face[...] = jnp.dot(slot_ref[...], pick, preferred_element_type=f32).astype(bf16)
+
+    load_rows[1].wait()
+    load_rows[2].wait()
+    hot16 = hot_ref[...].astype(bf16)
+    slots = slot_ref[...]
+    stack = []
+    for q in range(2):
+        stack += split(param_ref[q:q + 1, :], 2)
+    for q in range(2):
+        stack.append(span_ref[q:q + 1, :].astype(f32).astype(bf16))
+    out = nt_dot(jnp.concatenate([hot16 * part for part in stack], axis=0), slots)
+    out = [out[i * n:(i + 1) * n] for i in range(6)]
+    meta_send[:, 0, :] = out[0] + out[1]
+    meta_send[:, 1, :] = out[2] + out[3]
+    meta_send[:, 2, :] = out[4]
+    meta_send[:, 3, :] = out[5]
+    send_all(*meta)
 
     for side in (0, 1, 2, 3):
         take_face(1, side)
@@ -424,20 +452,6 @@
         send_face(2, side)
     add_values(1, val)
     sweep(val, field, y2, None)
-    hot16 = hot_ref[...].astype(bf16)
-    slots = slot_ref[...]
-    stack = []
-    for q in range(2):
-        stack += split(param_ref[q:q + 1, :], 2)
-    for q in range(2):
-        stack.append(span_ref[q:q + 1, :].astype(f32).astype(bf16))
-    out = nt_dot(jnp.concatenate([hot16 * part for part in stack], axis=0), slots)
-    out = [out[i * n:(i + 1) * n] for i in range(6)]
-    meta_send[:, 0, :] = out[0] + out[1]
-    meta_send[:, 1, :] = out[2] + out[3]
-    meta_send[:, 2, :] = out[4]
-    meta_send[:, 3, :] = out[5]
-    send_all(*meta)
 
 
     def surface(ix, carry):
@@ -563,9 +577,9 @@
         in_specs=[
             pl.BlockSpec(memory_space=pl.ANY),
             pl.BlockSpec(memory_space=pl.ANY),
-            pl.BlockSpec(memory_space=pltpu.VMEM),
-            pl.BlockSpec(memory_space=pltpu.VMEM),
-            pl.BlockSpec(memory_space=pltpu.VMEM),
+            pl.BlockSpec(memory_space=pl.ANY),
+            pl.BlockSpec(memory_space=pl.ANY),
+            pl.BlockSpec(memory_space=pl.ANY),
         ],
         out_specs=(vmem,) * 4,
         scratch_shapes=[
@@ -591,10 +605,13 @@
             pltpu.VMEM((4, cy, nz), f32),
             pltpu.VMEM((n, LANES), f32),
             pltpu.VMEM((LANES, LANES), bf16),
+            pltpu.VMEM((1, rows), jnp.int32),
+            pltpu.VMEM((2, rows), jnp.int32),
+            pltpu.VMEM((2, rows), f32),
             pltpu.VMEM((n, 4, LANES), f32),
             pltpu.VMEM((n, 4, LANES), f32),
             pltpu.VMEM((n, 4, LANES), f32),
-            dma((4,)),
+            dma((7,)),
             dma((12,)),
             dma((12,)),
             dma((4,)),

time: 29.3 us -> 28.6 us (0.976)
  Pallas kernels: 28.4 us -> 27.8 us
    pallas_call x1, Pallas kernels: 26.5 us -> 25.9 us  [body(): pl.pallas_call(functools.partial(kernel, (ngx, ngy, cx, cy, rows)), out_s...]
where the time goes in v5:
time: 28.6 us; the launch traced here: 28.4 us
  Pallas kernels  27.8 us (97%)
  between operations  0.64 us (2%)
    pallas_call x1, Pallas kernels, body(): pl.pallas_call(functools.partial(kernel, (ngx, ngy, cx, cy, rows)), out_s...  25.9 us
    pallas_call x1, Pallas kernels, body(): pl.pallas_call(functools.partial(product, n), out_shape=(jax.ShapeDtypeSt...  1.85 us

profile of v5, /device:TPU:0, one launch (start us, length us, event | category | flops | bytes accessed | tf_op | source)
XLA Modules:
  0.0 28.4 jit_solution(10285106502460546383)
XLA Ops:
  0.6 25.9 %shard_map.68 = (f32[3,1024,128]{2,1,0:T(8,128)S(1)}, f32[32,4,128]{2,1,0:T(4,128)S(1)}, f32[64,4096]{1,0:T(8,128)S(1)}, bf16[128,4096]{1,0:T(8,128)(2,1)S(1)}) custom-call(f32[3,1024,128]{2,1,0:T(8,128)} %bitcast.11, f32[1024,128]{1,0:T(8,128)} %bitcast.12, s32[1,1024]{1,0:T(1,128)} %bitcast.15, s32[2,1024]{1,0:T(2,128)} %bitcast.13, f32[2,1024]{1,0:T(2,128)} %bitcast.14), custom_call_target="tpu_custom_call" | custom-call | tf_op jit(solution)/shard_map/pallas_call | solution.py:569
  26.6 1.8 %shard_map.69 = (f32[3,1024,128]{2,1,0:T(8,128)}, f32[3,64,64]{2,1,0:T(8,128)}) custom-call(f32[3,1024,128]{2,1,0:T(8,128)S(1)} %get-tuple-element.8.val, f32[32,4,128]{2,1,0:T(4,128)S(1)} %get-tuple-element.9.surf_ref, f32[64,4096]{1,0:T(8,128)S(1)} %get-tuple-element.10.bu_ref, bf16[128,4096]{1,0:T(8,128)(2,1)S(1)} %get-tuple-element.11.bv_ref), custom_call_target="tpu_custom_call" | custom-call | tf_op jit(solution)/shard_map/pallas_call | solution.py:634

commit v6 on v5

--- a/solution.py
+++ b/solution.py
@@ -81,7 +81,7 @@
         pl.semaphore_signal(barrier, inc=1, device_id=(to // ngy, lax.rem(to, ngy)), device_id_type=MESH)
         return carry
 
-    lax.fori_loop(1, n, greet, 0)
+    lax.fori_loop(1, n, greet, 0, unroll=True)
 
     sides = (
         (gx > 0, (jnp.maximum(gx - 1, 0), gy), 1),
@@ -225,7 +225,7 @@
             all_copy(src, dst, sems, lax.rem(me + i, n), me).start()
             return carry
 
-        lax.fori_loop(1, n, go, 0)
+        lax.fori_loop(1, n, go, 0, unroll=True)
         dst[me] = src[me]
 
     def every(src, dst, sems):
@@ -294,12 +294,22 @@
                 for d in (step, -step, 1, -1):
                     weight = center + cpad[pl.ds(ct + d, cy), :]
                     total = total + weight[None] * ysrc[:, pl.ds(at + d, cy), :]
-                new = vol[:, pl.ds(to, cy), :] + (1.0 - OMEGA) * vsrc[:, pl.ds(to, cy), :] + total
+                new = vol[:, pl.ds(to, cy), :]
+                if vsrc is None:
+                    new = (2.0 - OMEGA) * new + total
+                else:
+                    new = new + (1.0 - OMEGA) * vsrc[:, pl.ds(to, cy), :] + total
                 done.append((at, to, new))
             for at, to, new in done:
                 vdst[:, pl.ds(to, cy), :] = new
                 if ydst is not None:
                     ydst[:, pl.ds(at, cy), :] = new * rd[pl.ds(to, cy), :][None]
+                else:
+                    lane = lax.broadcasted_iota(jnp.int32, (cy, LANES), 1)
+                    out = jnp.where(lane == 1, pltpu.roll(new[1], 1, 1), new[0])
+                    out = jnp.where(lane == 2, pltpu.roll(new[2], 2, 1), out)
+                    inv = rd[pl.ds(to, cy), :][:, 0:1] * OMEGA
+                    xcol[pl.ds(to, cy), :] = out * inv
             return carry
 
         lax.fori_loop(0, cx // UNROLL, layers, 0)
@@ -331,7 +341,7 @@
             total = up * pltpu.roll(mid, LANES - 1, 1) + pltpu.roll(up * mid, 1, 1)
             for d, weight in weights:
                 total = total + weight * y0[k, yl(d), :]
-            done.append(first + (1.0 - OMEGA) * first + total)
+            done.append((2.0 - OMEGA) * first + total)
         for k in range(3):
             field[k, flat, :] = done[k]
             y1[k, yl(0), :] = done[k] * inv
@@ -359,7 +369,7 @@
             for k in range(3):
                 dst[k, flat, :] = dst[k, flat, :] + face_w[side] * recv23[turn - 1, side, k]
 
-    sweep(vol, field, y0, y1)
+    sweep(None, field, y0, y1)
     for side in range(4):
         @pl.when(sides[side][0])
         def _(side=side):
@@ -454,17 +464,6 @@
     sweep(val, field, y2, None)
 
 
-    def surface(ix, carry):
-        to = pl.ds(pl.multiple_of(ix * cy, 8), cy)
-        lane = lax.broadcasted_iota(jnp.int32, (cy, LANES), 1)
-        inv = rd[to, :] * OMEGA
-        out = jnp.where(lane == 0, field[0, to, :] * inv, 0.0)
-        for k in (1, 2):
-            out = jnp.where(lane == k, pltpu.roll(field[k, to, :] * inv, k, 1), out)
-        xcol[to, :] = out
-        return carry
-
-    lax.fori_loop(0, cx, surface, 0, unroll=UNROLL)
     surf_rows = jnp.concatenate(
         [xcol[c * LANES:(c + 1) * LANES, :].T[0:8] for c in range(rows // LANES)], axis=1
     )

time: 28.6 us -> 28.3 us (0.990)
  Pallas kernels: 27.8 us -> 27.5 us
where the time goes in v6:
time: 28.3 us; the launch traced here: 28.2 us
  Pallas kernels  27.5 us (97%)
  between operations  0.64 us (2%)
    pallas_call x1, Pallas kernels, body(): pl.pallas_call(functools.partial(kernel, (ngx, ngy, cx, cy, rows)), out_s...  25.7 us
    pallas_call x1, Pallas kernels, body(): pl.pallas_call(functools.partial(product, n), out_shape=(jax.ShapeDtypeSt...  1.85 us

profile of v6, /device:TPU:0, one launch (start us, length us, event | category | flops | bytes accessed | tf_op | source)
XLA Modules:
  0.0 28.2 jit_solution(15201373922951230104)
XLA Ops:
  0.6 25.7 %shard_map.68 = (f32[3,1024,128]{2,1,0:T(8,128)S(1)}, f32[32,4,128]{2,1,0:T(4,128)S(1)}, f32[64,4096]{1,0:T(8,128)S(1)}, bf16[128,4096]{1,0:T(8,128)(2,1)S(1)}) custom-call(f32[3,1024,128]{2,1,0:T(8,128)} %bitcast.11, f32[1024,128]{1,0:T(8,128)} %bitcast.12, s32[1,1024]{1,0:T(1,128)} %bitcast.15, s32[2,1024]{1,0:T(2,128)} %bitcast.13, f32[2,1024]{1,0:T(2,128)} %bitcast.14), custom_call_target="tpu_custom_call" | custom-call | tf_op jit(solution)/shard_map/pallas_call | solution.py:568
  26.3 1.8 %shard_map.69 = (f32[3,1024,128]{2,1,0:T(8,128)}, f32[3,64,64]{2,1,0:T(8,128)}) custom-call(f32[3,1024,128]{2,1,0:T(8,128)S(1)} %get-tuple-element.8.val, f32[32,4,128]{2,1,0:T(4,128)S(1)} %get-tuple-element.9.surf_ref, f32[64,4096]{1,0:T(8,128)S(1)} %get-tuple-element.10.bu_ref, bf16[128,4096]{1,0:T(8,128)(2,1)S(1)} %get-tuple-element.11.bv_ref), custom_call_target="tpu_custom_call" | custom-call | tf_op jit(solution)/shard_map/pallas_call | solution.py:633
